TPU v7x, 32 devices: a whole 2x2x4 slice. The times are simulated.
32 devices in a mesh: row: 8 (over z, x), col: 4 (over y, core).
Axes of the slice: x: 2, y: 2, z: 4, core: 2. Of those that a mesh axis runs over, the one named last changes fastest.
Arguments:
- blocks: float32 [2048, 4, 128, 128], P(('row', 'col')), may hold values from -0.25 to 0.25
- block_cols: int32 [2048, 4], P(('row', 'col')), may hold values from 0 to 255, as said below
- targets: float32 [32, 262144], P(None, ('row', 'col')), may hold values from -6 to 6
Outputs:
- solution: float32 [32, 32768], P(None, ('row', 'col'))
- residual: float32 [32, 262144], P(None, ('row', 'col'))
Inputs may be any that keep to these rules, and one draw needn't show every extreme that they name: `block_cols`: the four indices of a block row differ. Block row i belongs to device d = i // 64, devices numbered row-major over (row, col); every index j of it satisfies (j // 8) % 4 == d % 4.
All inputs are finite; a program needn't handle non-finite values.
Results may differ from a plain program's by a relative error of at most 0.00012.
Values sent between devices are 32-bit elements; how exact they have to be, the bound alone decides.
No kernel may reach another device: no remote copies, remote signals or barrier semaphores. Data moves between devices by JAX's collectives and lax.ppermute only.
A program may use at most 128 MiB of HBM per device.

v0:
```python
import jax
import jax.numpy as jnp
from jax import lax
from jax.sharding import PartitionSpec as P

ITERS = 3
CBD = 8


def chol_solve(matrix, right):
    lower_factor = jnp.linalg.cholesky(matrix)
    middle = lax.linalg.triangular_solve(lower_factor, right, left_side=True, lower=True)
    return lax.linalg.triangular_solve(
        lower_factor, middle, left_side=True, lower=True, transpose_a=True
    )


def gram_of(matrix):
    return jnp.dot(
        matrix, matrix.T, precision=lax.Precision.HIGHEST, preferred_element_type=jnp.float32
    )


def body(blocks, block_cols, targets):
    row_count = lax.axis_size("row")
    col_count = lax.axis_size("col")
    block_rows = blocks.shape[0]
    tile_size = blocks.shape[2]
    rhs_count = targets.shape[0]
    group_size = CBD * row_count
    flat_cols = block_cols.reshape(-1)
    local_cols = flat_cols // CBD // col_count * CBD + flat_cols % CBD

    def backward(resid):
        shaped = resid.reshape(rhs_count, block_rows, tile_size)
        pieces_all = jnp.einsum("ikab,nia->iknb", blocks, shaped, precision=lax.Precision.HIGHEST)
        pieces_all = pieces_all.reshape(block_rows * 4, rhs_count, tile_size)
        summed = jax.ops.segment_sum(pieces_all, local_cols, num_segments=group_size)
        return summed.transpose(1, 0, 2).reshape(rhs_count, group_size * tile_size)

    def gradient_of(resid):
        gradient = lax.psum(backward(resid), "row")
        total_gram = lax.psum(gram_of(gradient), "col")
        return (gradient, total_gram)

    residual = targets
    gradient, grad_gram = gradient_of(residual)
    direction = gradient
    solution = jnp.zeros(direction.shape, jnp.float32)
    for iteration in range(ITERS):
        gathered = direction
        tiles = gathered.reshape(rhs_count, group_size, tile_size)
        picked = jnp.take(tiles, local_cols, axis=1).reshape(rhs_count, block_rows, 4, tile_size)
        image = jnp.einsum("ikab,nikb->nia", blocks, picked, precision=lax.Precision.HIGHEST)
        image = image.reshape(rhs_count, block_rows * tile_size)
        image_gram = lax.psum(gram_of(image), ("row", "col"))
        step_size = chol_solve(image_gram, grad_gram)
        solution = solution + jnp.dot(step_size.T, direction, precision=lax.Precision.HIGHEST)
        residual = residual - jnp.dot(step_size.T, image, precision=lax.Precision.HIGHEST)
        if iteration + 1 < ITERS:
            gradient, new_gram = gradient_of(residual)
            mix = chol_solve(grad_gram, new_gram)
            direction = gradient + jnp.dot(mix.T, direction, precision=lax.Precision.HIGHEST)
            grad_gram = new_gram
    width = CBD * tile_size
    solution = lax.dynamic_slice_in_dim(solution, lax.axis_index("row") * width, width, 1)
    return (solution, residual)


def solution(mesh):
    placed = (P(("row", "col"), None, None, None), P(("row", "col"), None), P(None, ("row", "col")))
    return jax.shard_map(
        body,
        mesh=mesh,
        in_specs=placed,
        out_specs=(P(None, ("row", "col")), P(None, ("row", "col"))),
        check_vma=False,
    )
```

profile of v0, /device:TPU:0, one launch (start us, length us, event | category | flops | bytes accessed | tf_op | source)
XLA Modules:
  0.0 638.0 jit_solution(16200924046019164023)
XLA Ops:
  9.5 13.1 %fusion.13 = f32[64,32,4,128]{3,1,2,0:T(8,128)} fusion(f32[64,4,128,128]{3,2,1,0:T(8,128)} %param.10, f32[32,64,128,1]{2,1,0,3:T(8,128)S(1)} %bitcast.221), kind=kOutput, calls=%fused_computation.36 | convolution fusion | flops 1610612736 | bytes 22020096 | tf_op jit(solution)/shard_map/ikab,nia->iknb/dot_general | solution.py:36
  22.7 22.4 %scatter_fusion = f32[64,32,128]{2,1,0:T(8,128)S(1)} fusion(f32[64,32,128]{2,1,0:T(8,128)S(1)} %broadcast.181.clone, s32[256]{0:T(256)S(1)} %bitcast.224, f32[256,32,128]{2,1,0:T(8,128)} %bitcast.213), kind=kCustom, calls=%fused_computation.3 | custom fusion | flops 1048576 | bytes 12583936 | tf_op jit(solution)/shard_map/scatter-add | solution.py:38
  46.4 80.8 %all-reduce.4.cloned.1.call-done = f32[32,8192]{1,0:T(8,128)} async-done(((f32[32,8192]{1,0:T(8,128)}), f32[32,8192]{1,0:T(8,128)}) %all-reduce.4.cloned.1.call-update) | async-done | bytes 1048592 | tf_op jit(solution)/shard_map/psum | solution.py:42
  128.6 3.0 gather_fusion
  131.5 2.7 broadcast_select_fusion.2
  134.3 19.4 %fusion.47 = f32[64,32,128,1]{2,1,3,0:T(8,128)S(1)} fusion(f32[32,64,4,128]{3,0,2,1:T(8,128)S(1)} %bitcast.216, f32[64,4,128,128]{3,2,1,0:T(8,128)} %param.10), kind=kOutput, calls=%fused_computation.115 | convolution fusion | flops 1610612736 | bytes 22020096 | tf_op jit(solution)/shard_map/ikab,nikb->nia/dot_general | solution.py:54
  154.7 39.8 %psum.64 = f32[32,32]{0,1:T(8,128)S(1)} all-reduce(f32[32,32]{0,1:T(8,128)S(1)} %convolution_bitcast_fusion.2), channel_id=1, replica_groups=mesh['row'=8,'col'=4] {'row','col'}, use_global_device_ids=true, to_apply=%region_2.4 | all-reduce | flops 1024 | bytes 8192 | tf_op jit(solution)/shard_map/psum | solution.py:56
  194.5 2.9 cholesky.89
  198.8 2.4 custom-call.17
  202.2 10.4 %psum.65 = f32[32,32]{0,1:T(8,128)S(1)} all-reduce(f32[32,32]{0,1:T(8,128)S(1)} %fusion.48), channel_id=1, replica_groups=mesh['row'=8,'col'=4] {'col'}, use_global_device_ids=true, to_apply=%region_5.8 | all-reduce | flops 1024 | bytes 8192 | tf_op jit(solution)/shard_map/psum | solution.py:43
  215.2 13.1 %fusion.10 = f32[64,32,4,128]{3,1,2,0:T(8,128)} fusion(f32[64,4,128,128]{3,2,1,0:T(8,128)} %param.10, f32[32,64,128,1]{2,1,0,3:T(8,128)S(1)} %bitcast.222), kind=kOutput, calls=%fused_computation.33 | convolution fusion | flops 1610612736 | bytes 22020096 | tf_op jit(solution)/shard_map/ikab,nia->iknb/dot_general | solution.py:36
  228.4 22.4 %scatter_fusion.1 = f32[64,32,128]{2,1,0:T(8,128)S(1)} fusion(f32[64,32,128]{2,1,0:T(8,128)S(1)} %broadcast.181.clone.1, s32[256]{0:T(256)S(1)} %bitcast.225, f32[256,32,128]{2,1,0:T(8,128)} %bitcast.214), kind=kCustom, calls=%fused_computation.4 | custom fusion | flops 1048576 | bytes 12583936 | tf_op jit(solution)/shard_map/scatter-add | solution.py:38
  252.1 2.9 cholesky.100
  258.8 70.6 %all-reduce.6.cloned.1.call-done = f32[32,8192]{1,0:T(8,128)} async-done(((f32[32,8192]{1,0:T(8,128)}), f32[32,8192]{1,0:T(8,128)}) %all-reduce.6.cloned.1.call-update) | async-done | bytes 1048592 | tf_op jit(solution)/shard_map/psum | solution.py:42
  329.4 2.5 fusion.50
  331.9 10.2 %psum.67 = f32[32,32]{0,1:T(8,128)S(1)} all-reduce(f32[32,32]{0,1:T(8,128)S(1)} %fusion.50), channel_id=1, replica_groups=mesh['row'=8,'col'=4] {'col'}, use_global_device_ids=true, to_apply=%region_8.13 | all-reduce | flops 1024 | bytes 8192 | tf_op jit(solution)/shard_map/psum | solution.py:43
  344.9 3.0 gather_fusion.1
  347.9 2.7 broadcast_select_fusion.1
  350.6 19.4 %fusion.51 = f32[64,32,128,1]{2,1,3,0:T(8,128)S(1)} fusion(f32[32,64,4,128]{3,0,2,1:T(8,128)S(1)} %bitcast.217, f32[64,4,128,128]{3,2,1,0:T(8,128)} %param.10), kind=kOutput, calls=%fused_computation.119 | convolution fusion | flops 1610612736 | bytes 22020096 | tf_op jit(solution)/shard_map/ikab,nikb->nia/dot_general | solution.py:54
  372.0 40.0 %psum.68 = f32[32,32]{0,1:T(8,128)S(1)} all-reduce(f32[32,32]{0,1:T(8,128)S(1)} %convolution_bitcast_fusion.1), channel_id=1, replica_groups=mesh['row'=8,'col'=4] {'row','col'}, use_global_device_ids=true, to_apply=%region_9.14 | all-reduce | flops 1024 | bytes 8192 | tf_op jit(solution)/shard_map/psum | solution.py:56
  412.1 2.9 cholesky.111
  422.6 13.1 %fusion.7 = f32[64,32,4,128]{3,1,2,0:T(8,128)} fusion(f32[64,4,128,128]{3,2,1,0:T(8,128)} %param.10, f32[32,64,128,1]{2,1,0,3:T(8,128)S(1)} %bitcast.223), kind=kOutput, calls=%fused_computation.30 | convolution fusion | flops 1610612736 | bytes 22020096 | tf_op jit(solution)/shard_map/ikab,nia->iknb/dot_general | solution.py:36
  435.8 22.4 %scatter_fusion.2 = f32[64,32,128]{2,1,0:T(8,128)S(1)} fusion(f32[64,32,128]{2,1,0:T(8,128)S(1)} %broadcast.181, s32[256]{0:T(256)S(1)} %bitcast.226, f32[256,32,128]{2,1,0:T(8,128)} %bitcast.212), kind=kCustom, calls=%fused_computation.5 | custom fusion | flops 1048576 | bytes 12583936 | tf_op jit(solution)/shard_map/scatter-add | solution.py:38
  461.4 2.9 cholesky.122
  470.2 67.3 %all-reduce.8.cloned.1.call-done = f32[32,8192]{1,0:T(8,128)} async-done(((f32[32,8192]{1,0:T(8,128)}), f32[32,8192]{1,0:T(8,128)}) %all-reduce.8.cloned.1.call-update) | async-done | bytes 1048592 | tf_op jit(solution)/shard_map/psum | solution.py:42
  537.4 2.5 fusion.53
  540.0 10.5 %psum.70 = f32[32,32]{1,0:T(8,128)S(1)} all-reduce(f32[32,32]{1,0:T(8,128)S(1)} %fusion.53), channel_id=1, replica_groups=mesh['row'=8,'col'=4] {'col'}, use_global_device_ids=true, to_apply=%region_12.17 | all-reduce | flops 1024 | bytes 8192 | tf_op jit(solution)/shard_map/psum | solution.py:43
  553.3 3.0 gather_fusion.2
  556.2 2.7 broadcast_select_fusion
  559.0 19.4 %fusion.54 = f32[64,32,128,1]{2,1,3,0:T(8,128)S(1)} fusion(f32[32,64,4,128]{3,0,2,1:T(8,128)S(1)} %bitcast.215, f32[64,4,128,128]{3,2,1,0:T(8,128)} %param.10), kind=kOutput, calls=%fused_computation.122 | convolution fusion | flops 1610612736 | bytes 22020096 | tf_op jit(solution)/shard_map/ikab,nikb->nia/dot_general | solution.py:54
  579.4 39.8 %psum.71 = f32[32,32]{0,1:T(8,128)S(1)} all-reduce(f32[32,32]{0,1:T(8,128)S(1)} %convolution_bitcast_fusion), channel_id=1, replica_groups=mesh['row'=8,'col'=4] {'row','col'}, use_global_device_ids=true, to_apply=%region_13.18 | all-reduce | flops 1024 | bytes 8192 | tf_op jit(solution)/shard_map/psum | solution.py:56
  619.2 2.9 cholesky.133
  (90 shorter events, 50.1 us)
Async XLA Ops:
  7.2 120.0 %all-reduce.4.cloned.1.call-start = ((), (), s32[]{:S(2)}) async-start(), calls=%async_computation | async-start | bytes 2097152 | tf_op jit(solution)/shard_map/psum | solution.py:42
  46.2 283.2 %all-reduce.6.cloned.1.call-start = ((), (), s32[]{:S(2)}) async-start(), calls=%async_computation.1 | async-start | bytes 2097152 | tf_op jit(solution)/shard_map/psum | solution.py:42
  134.3 67.0 %copy-start = (f32[32,8192]{1,0:T(8,128)S(1)}, f32[32,8192]{1,0:T(8,128)}, u32[]{:S(2)}) copy-start(f32[32,8192]{1,0:T(8,128)} %all-reduce.4.cloned.1.call-done) | copy-start | bytes 3145732
  153.7 59.3 %copy-start.6 = (f32[32,8192]{1,0:T(8,128)S(1)}, f32[32,8192]{1,0:T(8,128)}, u32[]{:S(2)}) copy-start(f32[32,8192]{1,0:T(8,128)} %param.12) | copy-start | bytes 3145732
  214.1 1.0 copy-start.1
  252.0 285.5 %all-reduce.8.cloned.1.call-start = ((), (), s32[]{:S(2)}) async-start(), calls=%async_computation.2 | async-start | bytes 2097152 | tf_op jit(solution)/shard_map/psum | solution.py:42
  350.6 68.6 %copy-start.2 = (f32[32,8192]{1,0:T(8,128)S(1)}, f32[32,8192]{1,0:T(8,128)}, u32[]{:S(2)}) copy-start(f32[32,8192]{1,0:T(8,128)} %copy-done.1) | copy-start | bytes 3145732
  370.0 1.0 copy-start.5
  421.4 1.0 copy-start.3
  559.0 67.4 %copy-start.4 = (f32[32,8192]{1,0:T(8,128)S(1)}, f32[32,8192]{1,0:T(8,128)}, u32[]{:S(2)}) copy-start(f32[32,8192]{1,0:T(8,128)} %copy-done.3) | copy-start | bytes 3145732
Sparse Core Ops, SparseCore 0:
  46.3 80.8 all-reduce.3
  252.1 77.2 all-reduce.5
  459.4 77.9 all-reduce.7
where the time goes:
time: 648 us; the launch traced here: 638 us
  waiting for transfers between devices  219 us (34%)
  blocking collectives  151 us (23%)
  matrix products  123 us (19%)
  other arithmetic  111 us (17%)
  local copies, waits for them, and re-layouts  20.1 us (3%)
  between operations  14.6 us (2%)
    psum x3, waiting for transfers between devices, gradient_of(): gradient = lax.psum(backward(resid), 'row')  219 us
    psum x3, blocking collectives, body(): image_gram = lax.psum(gram_of(image), ('row', 'col'))  120 us
    scatter-add x3, other arithmetic, backward(): jax.ops.segment_sum(pieces_all, local_cols, num_segments=group_size)  67.3 us
    dot_general x3, matrix products, body(): jnp.einsum('ikab,nikb->nia', blocks, picked, precision=lax.Precision.HIGH...  58.3 us
    dot_general x3, matrix products, backward(): jnp.einsum('ikab,nia->iknb', blocks, shaped, precision=lax.Precision.HIGH...  39.2 us
    psum x3, blocking collectives, gradient_of(): total_gram = lax.psum(gram_of(gradient), 'col')  31.2 us
    another operation x15, other arithmetic, chol_solve(): lower_factor = jnp.linalg.cholesky(matrix)  18 us
    another operation x10, other arithmetic, chol_solve(): lax.linalg.triangular_solve(lower_factor, middle, left_side=True, lower=T...  15.4 us
  transfers between devices with their start and end apart: 3, of which 3 were waited for; matrix products, arithmetic and copies ran while one was open for 3% of the time, Pallas kernels for 0%

commit v1 on v0

v1 whole, which is shorter than its diff:
```python
import functools

import jax
import jax.numpy as jnp
from jax import lax
from jax.experimental import pallas as pl
from jax.experimental.pallas import tpu as pltpu
from jax.sharding import PartitionSpec as P

CBD = 8
COPY_ROWS = 4
STEP_ROWS = 16
MIB = 1024 * 1024
F32 = jnp.float32
BF16 = jnp.bfloat16


def split(value):
    high = value.astype(BF16)
    return high, (value - high.astype(F32)).astype(BF16)


def stack(value):
    return jnp.concatenate(split(value), axis=0)


def dot_last(left, right):
    return lax.dot_general(left, right, (((1,), (1,)), ((), ())), preferred_element_type=F32)


def dot_first(left, right):
    return lax.dot_general(left, right, (((1,), (0,)), ((), ())), preferred_element_type=F32)


def dot_small(left, right, left_dim):
    return lax.dot_general(
        left,
        right,
        (((left_dim,), (0,)), ((), ())),
        precision=lax.Precision.HIGHEST,
        preferred_element_type=F32,
    )


def fold(product):
    rows, lanes = product.shape[0] // 2, product.shape[1] // 2
    return product[:rows, :lanes] + (
        product[:rows, lanes:] + product[rows:, :lanes] + product[rows:, lanes:]
    )


def tile_at(index, tile):
    return pl.ds(pl.multiple_of(index * tile, tile), tile)


def backward_piece(cols_ref, row, weights, parts, sums_ref):
    rhs = parts.shape[0] // 2
    tile = parts.shape[1]
    product = dot_first(jnp.concatenate([parts, parts], axis=1), weights)
    product = product[:rhs] + product[rhs:]
    for k in range(4):
        at = cols_ref[row * 4 + k]
        sums_ref[at] = sums_ref[at] + product[:, k * tile : (k + 1) * tile]


def forward_piece(cols_ref, row, weights, halves_ref):
    picked = jnp.concatenate([halves_ref[cols_ref[row * 4 + k]] for k in range(4)], axis=1)
    return fold(dot_last(picked, weights))


def combine(coefficient_parts, high, low):
    rows = coefficient_parts.shape[0] // 2
    product = dot_first(coefficient_parts, high)
    return product[:rows] + (product[rows:] + dot_first(coefficient_parts[:rows], low))


def fill_halves(vector_refs, halves_ref):
    base = 0
    for vector_ref in vector_refs:

        @pl.loop(0, vector_ref.shape[0], unroll=CBD)
        def _(j):
            halves_ref[base + j] = stack(vector_ref[j])

        base += vector_ref.shape[0]


def empty_sums(sums_ref):
    @pl.loop(0, sums_ref.shape[0], unroll=CBD)
    def _(j):
        sums_ref[j] = jnp.zeros(sums_ref.shape[1:], F32)


def hand_out(sums_ref, share_refs, grams=None):
    size = CBD + int(grams is not None)
    slot = 0
    for share_ref in share_refs:
        for part in range(share_ref.shape[0] // size):

            @pl.loop(0, CBD, unroll=CBD)
            def _(j):
                share_ref[part * size + j] = sums_ref[slot * CBD + j]

            if grams is not None:
                share_ref[part * size + CBD] = grams
            slot += 1


def prepare_kernel(cols_ref, blocks_ref, source_ref, weights_ref, *refs):
    share_refs, (staged_ref, value_ref, sums_ref, semaphores) = refs[:-4], refs[-4:]
    chunks = blocks_ref.shape[0] // COPY_ROWS
    tile = blocks_ref.shape[-1]

    def copy(chunk):
        rows = pl.ds(chunk * COPY_ROWS, COPY_ROWS)
        return pltpu.make_async_copy(
            blocks_ref.at[rows], staged_ref.at[rows], semaphores.at[chunk]
        )

    value_copy = pltpu.make_async_copy(source_ref, value_ref, semaphores.at[chunks])
    value_copy.start()

    @pl.loop(0, chunks)
    def _(chunk):
        copy(chunk).start()

    empty_sums(sums_ref)
    value_copy.wait()

    @pl.loop(0, chunks, step=2)
    def _(chunk):
        copy(chunk).wait()
        copy(chunk + 1).wait()
        for i in range(2 * COPY_ROWS):
            row = chunk * COPY_ROWS + i
            wide = jnp.concatenate([staged_ref[row, k] for k in range(4)], axis=1)
            weights = stack(wide)
            weights_ref[row] = weights
            backward_piece(cols_ref, row, weights, stack(value_ref[:, tile_at(row, tile)]), sums_ref)

    hand_out(sums_ref, share_refs)


def prepare(cols, blocks, value, groups):
    block_rows, _, tile, _ = blocks.shape
    rhs = value.shape[0]
    shares = [jax.ShapeDtypeStruct((count * CBD, rhs, tile), F32) for count in groups]
    vmem = pl.BlockSpec(memory_space=pltpu.VMEM)
    return pl.pallas_call(
        prepare_kernel,
        in_specs=[
            pl.BlockSpec(memory_space=pltpu.SMEM),
            pl.BlockSpec(memory_space=pl.ANY),
            pl.BlockSpec(memory_space=pl.ANY),
        ],
        out_specs=[vmem] * (1 + len(groups)),
        out_shape=[pltpu.VMEM((block_rows, 2 * tile, 4 * tile), BF16)] + shares,
        scratch_shapes=[
            pltpu.VMEM(blocks.shape, F32),
            pltpu.VMEM(value.shape, F32),
            pltpu.VMEM((sum(groups) * CBD, rhs, tile), F32),
            pltpu.SemaphoreType.DMA((block_rows // COPY_ROWS + 1,)),
        ],
        compiler_params=pltpu.CompilerParams(vmem_limit_bytes=24 * MIB),
        cost_estimate=pl.CostEstimate(
            flops=6 * blocks.size * rhs, bytes_accessed=blocks.size * 4, transcendentals=0
        ),
    )(
        cols,
        pltpu.with_memory_space_constraint(blocks, pltpu.HBM),
        pltpu.with_memory_space_constraint(value, pltpu.HBM),
    )


def sweep_kernel(inputs, outputs, mode, cols_ref, weights_ref, *refs):
    first, backward = mode == "first", mode != "last"
    vector_refs, refs = refs[:inputs], refs[inputs:]
    share_ref, refs = refs[0], refs[1:]
    if not first:
        base_ref, coefficient_ref, old_ref, refs = refs[0], refs[1], refs[2], refs[3:]
    image_ref, refs = refs[0], refs[1:]
    raw_ref = image_ref
    if mode == "middle":
        raw_ref, refs = refs[0], refs[1:]
    if backward:
        sum_refs, refs = refs[:outputs], refs[outputs:]
        sums_ref, refs = refs[0], refs[1:]
    else:
        gram_ref, refs = refs[0], refs[1:]
    halves_ref, parts_ref, products_ref = refs
    share, rhs, tile = share_ref.shape
    chunks = weights_ref.shape[0] // STEP_ROWS

    fill_halves(vector_refs, halves_ref)
    if backward:
        empty_sums(sums_ref)
    products_ref[...] = jnp.zeros_like(products_ref)
    if not first:
        coefficient_parts = stack(coefficient_ref[...].T)

    def ahead(chunk):
        for i in range(STEP_ROWS):
            row = chunk * STEP_ROWS + i
            value = forward_piece(cols_ref, row, weights_ref[row], halves_ref)
            if backward:
                raw_ref[:, tile_at(row, tile)] = value
            parts_ref[lax.rem(chunk, 2), :, i * tile : (i + 1) * tile] = stack(value)

    def behind(chunk):
        parts = parts_ref[lax.rem(chunk, 2)]
        at = tile_at(chunk, STEP_ROWS * tile)
        if first:
            left = right = parts
        else:
            image = base_ref[:, at] + combine(coefficient_parts, parts[:rhs], parts[rhs:])
            image_ref[:, at] = image
            right = stack(image)
            left = jnp.concatenate([right, stack(old_ref[:, at])], axis=0)
        products_ref[...] += dot_last(left, right)
        if backward:
            for i in range(STEP_ROWS):
                row = chunk * STEP_ROWS + i
                backward_piece(
                    cols_ref, row, weights_ref[row], parts[:, i * tile : (i + 1) * tile], sums_ref
                )

    ahead(0)

    @pl.loop(1, chunks)
    def _(chunk):
        ahead(chunk)
        behind(chunk - 1)

    behind(chunks - 1)
    own = jnp.concatenate([stack(share_ref[j]) for j in range(share)], axis=1)
    grams = [fold(dot_last(own, own)), fold(products_ref[: 2 * rhs])]
    if not first:
        grams.append(fold(products_ref[2 * rhs :]))
    grams.append(jnp.zeros((rhs, tile - len(grams) * rhs), F32))
    grams = jnp.concatenate(grams, axis=1)
    if backward:
        hand_out(sums_ref, sum_refs, grams)
    else:
        gram_ref[...] = grams


def sweep(cols, weights, vectors, groups, share, mode, extra=()):
    block_rows, _, width = weights.shape
    slots = sum(groups)
    _, rhs, tile = share.shape
    grams = 2 if mode == "first" else 3
    vmem = pl.BlockSpec(memory_space=pltpu.VMEM)
    wide = jax.ShapeDtypeStruct((rhs, block_rows * tile), F32)
    out_shape = [wide]
    scratch = [
        pltpu.VMEM((slots * CBD, 2 * rhs, tile), BF16),
        pltpu.VMEM((2, 2 * rhs, STEP_ROWS * tile), BF16),
        pltpu.VMEM(((grams - 1) * 2 * rhs, 2 * rhs), F32),
    ]
    if mode == "middle":
        out_shape.append(wide)
    if mode != "last":
        out_shape += [
            jax.ShapeDtypeStruct((count * (CBD + 1), rhs, tile), F32) for count in groups
        ]
        scratch = [pltpu.VMEM((slots * CBD, rhs, tile), F32)] + scratch
    else:
        out_shape.append(jax.ShapeDtypeStruct((rhs, tile), F32))
    operands = list(vectors) + [share] + list(extra)
    return pl.pallas_call(
        functools.partial(sweep_kernel, len(vectors), len(groups), mode),
        in_specs=[pl.BlockSpec(memory_space=pltpu.SMEM)] + [vmem] * (1 + len(operands)),
        out_specs=[vmem] * len(out_shape),
        out_shape=out_shape,
        scratch_shapes=scratch,
        compiler_params=pltpu.CompilerParams(vmem_limit_bytes=14 * MIB),
        cost_estimate=pl.CostEstimate(
            flops=6 * (1 + int(mode != "last")) * weights.size * rhs // 2,
            bytes_accessed=weights.size,
            transcendentals=0,
        ),
    )(cols, pltpu.with_memory_space_constraint(weights, pltpu.VMEM), *operands)


def eliminate(systems):
    size = systems[0][0].shape[0]
    row_ids = lax.broadcasted_iota(jnp.int32, (size, 1), 0)
    wides = [jnp.concatenate(pair, axis=1) for pair in systems]
    for k in range(0, size, 2):
        done = []
        for wide in wides:
            first = jnp.broadcast_to(wide[:, k : k + 1], wide.shape)
            second = jnp.broadcast_to(wide[:, k + 1 : k + 2], wide.shape)
            a, c = first[k : k + 1], first[k + 1 : k + 2]
            b, d = second[k : k + 1], second[k + 1 : k + 2]
            one, two = wide[k : k + 1], wide[k + 1 : k + 2]
            inverse = 1.0 / (a * d - b * c)
            top = (d * one - b * two) * inverse
            low = (a * two - c * one) * inverse
            rest = wide - first * top - second * low
            done.append(jnp.where(row_ids == k, top, jnp.where(row_ids == k + 1, low, rest)))
        wides = done
    return [wide[:, size:] for wide in wides]


def identity(size):
    rows = lax.broadcasted_iota(jnp.int32, (size, size), 0)
    lanes = lax.broadcasted_iota(jnp.int32, (size, size), 1)
    return jnp.where(rows == lanes, 1.0, 0.0).astype(F32)


def coefficients(grams, previous):
    rhs = grams.shape[0]
    own_gram = grams[:, :rhs]
    image_gram = grams[:, rhs : 2 * rhs]
    if previous is None:
        return own_gram, image_gram, None
    old_inverse, old_gram = previous
    cross = grams[:, 2 * rhs : 3 * rhs]
    mix = dot_small(old_inverse, own_gram, 1)
    image_gram = image_gram + (
        dot_small(mix, cross, 0)
        + dot_small(cross, mix, 0)
        + dot_small(mix, dot_small(old_gram, mix, 1), 0)
    )
    return own_gram, image_gram, mix


def added(refs):
    total = refs[0][...]
    for ref in refs[1:]:
        total = total + ref[...]
    return total


def first_steps_kernel(*refs):
    step_ref, inverse_ref, gram_ref, minus_ref = refs[-4:]
    own_gram, image_gram, _ = coefficients(added(refs[:-4]), None)
    step, inverse = eliminate([(image_gram, own_gram), (own_gram, identity(own_gram.shape[0]))])
    step_ref[...] = step
    inverse_ref[...] = inverse
    gram_ref[...] = image_gram
    minus_ref[...] = -step


def next_steps_kernel(*refs):
    old_step_ref, old_inverse_ref, old_gram_ref = refs[-9:-6]
    step_ref, inverse_ref, gram_ref, mix_ref, base_ref, raw_ref = refs[-6:]
    previous = (old_inverse_ref[...], old_gram_ref[...])
    own_gram, image_gram, mix = coefficients(added(refs[:-9]), previous)
    step, inverse = eliminate([(image_gram, own_gram), (own_gram, identity(own_gram.shape[0]))])
    step_ref[...] = step
    inverse_ref[...] = inverse
    gram_ref[...] = image_gram
    mix_ref[...] = mix
    base_ref[...] = -step - dot_small(mix, step, 1)
    raw_ref[...] = dot_small(old_step_ref[...], step, 1)


def cost(flops, elements):
    return pl.CostEstimate(flops=flops, bytes_accessed=4 * elements, transcendentals=0)


def small_call(kernel, count, *operands):
    rhs = operands[0].shape[0]
    return pl.pallas_call(
        kernel,
        out_shape=[jax.ShapeDtypeStruct((rhs, rhs), F32)] * count,
        compiler_params=pltpu.CompilerParams(vmem_limit_bytes=2 * MIB),
        cost_estimate=cost(4 * 10**9, MIB),
    )(*operands)


def whole(ref):
    return jnp.concatenate([ref[j] for j in range(ref.shape[0])], axis=1)


def place(ref, value):
    tile = ref.shape[2]
    for j in range(ref.shape[0]):
        ref[j] = value[:, j * tile : (j + 1) * tile]


def gradient_kernel(g1_ref, q0_ref, p0_ref, step0_ref, step1_ref, mix_ref, g2_ref):
    q0 = whole(q0_ref)
    normal = q0 - dot_small(step0_ref[...], whole(p0_ref), 0) + dot_small(mix_ref[...], q0, 0)
    place(g2_ref, whole(g1_ref) - dot_small(step1_ref[...], normal, 0))


def next_gradient(*operands):
    return pl.pallas_call(
        gradient_kernel,
        out_shape=jax.ShapeDtypeStruct(operands[0].shape, F32),
        compiler_params=pltpu.CompilerParams(vmem_limit_bytes=4 * MIB),
        cost_estimate=cost(10**9, MIB),
    )(*operands)


def solution_kernel(g0_ref, g1_ref, step0_ref, step1_ref, mix_ref, direction_ref, sol_ref):
    g0 = whole(g0_ref)
    direction = whole(g1_ref) + dot_small(mix_ref[...], g0, 0)
    place(direction_ref, direction)
    sol_ref[...] = dot_small(step0_ref[...], g0, 0) + dot_small(step1_ref[...], direction, 0)


def solution_so_far(g0, *operands):
    row = jax.ShapeDtypeStruct((g0.shape[1], g0.shape[0] * g0.shape[2]), F32)
    return pl.pallas_call(
        solution_kernel,
        out_shape=[jax.ShapeDtypeStruct(g0.shape, F32), row],
        compiler_params=pltpu.CompilerParams(vmem_limit_bytes=4 * MIB),
        cost_estimate=cost(10**9, MIB),
    )(g0, *operands)


def images_kernel(y0_ref, y1_ref, u0_ref, mix_ref, base_ref, image_ref, next_ref):
    of_y0 = stack(mix_ref[...].T)
    of_u0 = stack(base_ref[...].T)
    width = 1024

    @pl.loop(0, y0_ref.shape[1] // width)
    def _(i):
        at = tile_at(i, width)
        y1 = y1_ref[:, at]
        image_ref[:, at] = y1 + combine(of_y0, *split(y0_ref[:, at]))
        next_ref[:, at] = y1 + combine(of_u0, *split(u0_ref[:, at]))


def images(y0, *operands):
    return pl.pallas_call(
        images_kernel,
        out_shape=[jax.ShapeDtypeStruct(y0.shape, F32)] * 2,
        compiler_params=pltpu.CompilerParams(vmem_limit_bytes=12 * MIB),
        cost_estimate=cost(3 * 10**9, MIB),
    )(y0, *operands)


def residual_kernel(y0_ref, image_ref, targets_ref, step0_ref, step1_ref, resid_ref):
    parts = stack(-jnp.concatenate([step0_ref[...], step1_ref[...]], axis=0).T)
    width = 1024

    @pl.loop(0, y0_ref.shape[1] // width)
    def _(i):
        at = tile_at(i, width)
        pair = jnp.concatenate([y0_ref[:, at], image_ref[:, at]], axis=0)
        resid_ref[:, at] = targets_ref[:, at] + combine(parts, *split(pair))


def residual_so_far(y0, *operands):
    return pl.pallas_call(
        residual_kernel,
        out_shape=jax.ShapeDtypeStruct(y0.shape, F32),
        compiler_params=pltpu.CompilerParams(vmem_limit_bytes=12 * MIB),
        cost_estimate=cost(2 * 10**9, 2 * MIB),
    )(y0, *operands)


def finish_kernel(*refs):
    *gram_refs, inverse_ref, gram_ref, resid_ref, image_ref, old_image_ref = refs[:-7]
    share_ref, old_ref, sol_ref, out_sol_ref, out_ref, new_ref, semaphores = refs[-7:]
    previous = (inverse_ref[...], gram_ref[...])
    own_gram, image_gram, mix = coefficients(added(gram_refs), previous)
    (step,) = eliminate([(image_gram, own_gram)])
    tile = share_ref.shape[2]
    both = jnp.concatenate([step, dot_small(mix, step, 1)], axis=0)
    pairs = [jnp.concatenate([share_ref[j], old_ref[j]], axis=0) for j in range(share_ref.shape[0])]
    out_sol_ref[...] = sol_ref[...] + dot_small(both, jnp.concatenate(pairs, axis=1), 0)
    minus = stack(-both.T)
    width = resid_ref.shape[1] // semaphores.shape[0]
    copies = []
    for i in range(semaphores.shape[0]):
        at = slice(i * width, (i + 1) * width)
        pair = jnp.concatenate([image_ref[:, at], old_image_ref[:, at]], axis=0)
        new_ref[:, at] = resid_ref[:, at] + combine(minus, *split(pair))
        copies.append(
            pltpu.make_async_copy(new_ref.at[:, at], out_ref.at[:, at], semaphores.at[i])
        )
        copies[-1].start()
    for copy in copies:
        copy.wait()


def finish(grams, previous, resid, image, old_image, share, old_share, sol):
    vmem = pl.BlockSpec(memory_space=pltpu.VMEM)
    return pl.pallas_call(
        finish_kernel,
        in_specs=[vmem] * (len(grams) + len(previous) + 6),
        out_specs=[vmem, pl.BlockSpec(memory_space=pl.ANY)],
        scratch_shapes=[pltpu.VMEM(resid.shape, F32), pltpu.SemaphoreType.DMA((4,))],
        out_shape=[
            jax.ShapeDtypeStruct(sol.shape, F32),
            jax.ShapeDtypeStruct(resid.shape, F32),
        ],
        compiler_params=pltpu.CompilerParams(vmem_limit_bytes=12 * MIB),
    )(*grams, *previous, resid, image, old_image, share, old_share, sol)


def mixed(small, wide):
    return jnp.einsum("mn,jmb->jnb", small, wide, precision=lax.Precision.HIGHEST)


def sum_kernel(starts, *refs):
    parts, outs = refs[: len(starts)], refs[len(starts) :]
    size = outs[0].shape[0] + len(outs) - 1
    total = parts[0][starts[0] : starts[0] + size]
    for start, part in zip(starts[1:], parts[1:]):
        total = total + part[start : start + size]
    if len(outs) == 1:
        outs[0][...] = total
    else:
        outs[0][...] = total[: size - 1]
        outs[1][...] = total[size - 1]


def sum_of(parts, size, apart=False):
    rest = parts[0][0].shape[1:]
    if apart:
        out_shape = [jax.ShapeDtypeStruct((size - 1,) + rest, F32), jax.ShapeDtypeStruct(rest, F32)]
    else:
        out_shape = [jax.ShapeDtypeStruct((size,) + rest, F32)]
    out = pl.pallas_call(
        functools.partial(sum_kernel, [start for _, start in parts]),
        out_shape=out_shape,
        compiler_params=pltpu.CompilerParams(vmem_limit_bytes=4 * MIB),
    )(*[array for array, _ in parts])
    return out if apart else out[0]


def sum_whole(parts):
    return sum_of([(part, 0) for part in parts], parts[0].shape[0])


def join_kernel(*refs):
    size = refs[0].shape[0]
    for i, part in enumerate(refs[: refs[-1].shape[0] // size]):
        refs[-1][i * size : (i + 1) * size] = part[...]


def join(parts, after):
    shape = parts[0].shape
    vmem = pl.BlockSpec(memory_space=pltpu.VMEM)
    return pl.pallas_call(
        join_kernel,
        in_specs=[vmem] * len(parts) + [pl.BlockSpec(memory_space=pl.ANY)] * len(after),
        out_specs=vmem,
        out_shape=jax.ShapeDtypeStruct((len(parts) * shape[0],) + shape[1:], F32),
        compiler_params=pltpu.CompilerParams(vmem_limit_bytes=4 * MIB),
    )(*parts, *after)


class Ring:
    def __init__(self, count):
        self.nz = 4 if count % 4 == 0 else count
        self.nx = count // self.nz
        self.order = [0] + list(range(1, self.nz, 2)) + list(range(2, self.nz, 2))[::-1]

    def row(self, place, x):
        return self.order[place % self.nz] * self.nx + x % self.nx

    def next_z(self, value, by=1):
        pairs = [
            (self.row(p, x), self.row(p + by, x)) for p in range(self.nz) for x in range(self.nx)
        ]
        return lax.ppermute(value, "row", pairs)

    def next_x(self, value):
        pairs = [
            (self.row(p, x), self.row(p, x + 1)) for p in range(self.nz) for x in range(self.nx)
        ]
        return lax.ppermute(value, "row", pairs)

    def place_of(self, row):
        z = row // self.nx
        return jnp.where(z % 2 == 1, (z + 1) // 2, (self.nz - z // 2) % self.nz)

    def slot_of(self, row):
        me = lax.axis_index("row")
        back_z = (self.place_of(me) - self.place_of(row) + self.nz) % self.nz
        back_x = (me % self.nx - row % self.nx + self.nx) % self.nx
        return back_z * self.nx + back_x

    def along_x(self, share):
        pieces = [share]
        for _ in range(1, self.nx):
            pieces.append(self.next_x(pieces[-1]))
        return pieces

    def gather(self, share, after=()):
        row = self.along_x(share)
        arrays = list(row)
        for _ in range(self.nz // 2):
            share = self.next_z(share)
            last = [share, arrays[-1], *after]
            arrays += self.along_x(share)
        back = []
        for _ in range((self.nz - 1) // 2):
            back.insert(0, self.next_z(back[0] if back else join(row, last), -1))
        return arrays + back

    def groups(self):
        back = (self.nz - 1) // 2
        return [1] * self.nx + [self.nx] * back + [1] * (self.nx * (self.nz - 1 - back))

    def scatter(self, arrays, apart=False):
        steps_back = (self.nz - 1) // 2
        size = arrays[0].shape[0]
        own, arrays = arrays[: self.nx], arrays[self.nx :]
        backs, arrays = arrays[:steps_back], arrays[steps_back:]

        def over_x(slots):
            parts = []
            for t in list(range(1, self.nx)) + [0]:
                if parts:
                    whole = len(parts) == 1 and parts[0][0].shape[0] == size
                    parts = [(self.next_x(parts[0][0] if whole else sum_of(parts, size)), 0)]
                parts = parts + slots[t]
            return parts

        ahead = []
        for f in range(self.nz // 2, 0, -1):
            at = (self.nz - f - 1 - steps_back) * self.nx
            piece = sum_of(over_x([[(arrays[at + t], 0)] for t in range(self.nx)]), size)
            ahead.append((self.next_z(piece, f), 0))
        back = [self.next_z(backs[s - 1], -s) for s in range(steps_back, 0, -1)]
        here = [
            [(own[t], 0)] + [(array, t * size) for array in back] for t in range(self.nx)
        ]
        return sum_of(over_x(here) + ahead, size, apart)


def exchanges(axes):
    steps = []
    for axis in axes:
        bits = (lax.axis_size(axis) - 1).bit_length()
        while bits:
            taken = 2 if bits > 1 else 1
            bits -= taken
            steps.append((axis, [flip << bits for flip in range(1, 1 << taken)]))
    return steps


def sum_over(value, axes):
    parts = [value]
    for at, (axis, flips) in enumerate(exchanges(axes)):
        if at:
            value = sum_whole(parts)
        parts = [value]
        for flip in flips:
            pairs = [(i, i ^ flip) for i in range(lax.axis_size(axis))]
            parts.append(lax.ppermute(value, axis, pairs))
    return parts


def body(blocks, block_cols, targets):
    row_count = lax.axis_size("row")
    col_count = lax.axis_size("col")
    ring = Ring(row_count)
    owner = block_cols // CBD // col_count
    cols = (ring.slot_of(owner) * CBD + block_cols % CBD).reshape(-1)

    groups = ring.groups()
    weights, *sums = prepare(cols, blocks, targets, groups)
    g0 = ring.scatter(sums)

    y0, *sums = sweep(cols, weights, ring.gather(g0), groups, g0, "first")
    q0, grams = ring.scatter(sums, True)
    grams = sum_over(grams, ("col",))
    step0, inverse, image_gram, minus = small_call(first_steps_kernel, 4, *grams)

    g1 = g0 + mixed(minus, q0)
    y1, u0, *sums = sweep(
        cols, weights, ring.gather(q0, [step0]), groups, g1, "middle", (y0, minus, y0)
    )
    p0, grams = ring.scatter(sums, True)
    grams = sum_over(grams, ("col",))
    step1, inverse, image_gram, mix, of_u0, of_raw = small_call(
        next_steps_kernel, 6, *grams, step0, inverse, image_gram
    )

    g2 = next_gradient(g1, q0, p0, step0, step1, mix)
    image, base = images(y0, y1, u0, mix, of_u0)
    y2, grams = sweep(
        cols, weights, ring.gather(p0), groups, g2, "last", (base, of_raw, image)
    )
    grams = sum_over(grams, ("col", "row"))
    direction, solution = solution_so_far(g0, g1, step0, step1, mix)
    residual = residual_so_far(y0, image, targets, step0, step1)
    return finish(
        grams, (inverse, image_gram), residual, y2, image, g2, direction, solution
    )


def solution(mesh):
    placed = (P(("row", "col"), None, None, None), P(("row", "col"), None), P(None, ("row", "col")))
    return jax.shard_map(
        body,
        mesh=mesh,
        in_specs=placed,
        out_specs=(P(None, ("row", "col")), P(None, ("row", "col"))),
        check_vma=False,
    )
```

time: 648 us -> 172 us (0.27); the launches traced: 638 us -> 172 us
  waiting for transfers between devices: 219 us -> 58.6 us
  blocking collectives: 151 us -> 0 us
  matrix products: 123 us -> 0.31 us
  other arithmetic: 111 us -> 0.74 us
  starting transfers between devices: 0.12 us -> 60.1 us
  Pallas kernels: 0 us -> 51 us
  local copies, waits for them, and re-layouts: 20.1 us -> 0.21 us
  between operations: 14.6 us -> 1.08 us
    psum x3 -> x0, waiting for transfers between devices: 219 us -> none  [gradient_of(): gradient = lax.psum(backward(resid), 'row')]
    psum x6 -> x0, blocking collectives: 151 us -> none  [the longest x3 120 us: body(): image_gram = lax.psum(gram_of(image), ('row', 'col'))]
    dot_general x20 -> x1, matrix products: 121 us -> 0.31 us  [mixed(): jnp.einsum('mn,jmb->jnb', small, wide, precision=lax.Precision.HIGHEST)]
    scatter-add x3 -> x0, other arithmetic: 67.3 us -> none  [backward(): jax.ops.segment_sum(pieces_all, local_cols, num_segments=group_size)]
    ppermute x0 -> x49, starting transfers between devices: none -> 60.1 us  [the longest x18 25.2 us: next_z(): return lax.ppermute(value, 'row', pairs)]
    ppermute x0 -> x49, waiting for transfers between devices: none -> 58.6 us  [the longest x18 34.6 us: next_z(): return lax.ppermute(value, 'row', pairs)]
    pallas_call x0 -> x28, Pallas kernels: none -> 51 us  [the longest x3 29.3 us: sweep(): pl.pallas_call(functools.partial(sweep_kernel, len(vectors), len(groups),...]
    another operation x25 -> x0, other arithmetic: 33.4 us -> none  [the longest x15 18 us: chol_solve(): lower_factor = jnp.linalg.cholesky(matrix)]
  transfers between devices with their start and end apart: 3 -> 49, of which waited for: 3 -> 24; matrix products, arithmetic and copies ran while one was open for 3% -> 0% of each run, Pallas kernels for 0% -> 5%
where the time goes in v1:
time: 172 us
  starting transfers between devices  60.1 us (35%)
  waiting for transfers between devices  58.6 us (34%)
  Pallas kernels  51 us (30%)
    ppermute x18, waiting for transfers between devices, next_z(): return lax.ppermute(value, 'row', pairs)  34.6 us
    pallas_call x3, Pallas kernels, sweep(): pl.pallas_call(functools.partial(sweep_kernel, len(vectors), len(groups),...  29.3 us
    ppermute x18, starting transfers between devices, next_z(): return lax.ppermute(value, 'row', pairs)  25.2 us
    ppermute x18, starting transfers between devices, next_x(): return lax.ppermute(value, 'row', pairs)  23.5 us
    ppermute x18, waiting for transfers between devices, next_x(): return lax.ppermute(value, 'row', pairs)  19.3 us
    ppermute x13, starting transfers between devices, sum_over(): parts.append(lax.ppermute(value, axis, pairs))  11.4 us
    pallas_call x1, Pallas kernels, prepare(): pl.pallas_call(prepare_kernel, in_specs=[pl.BlockSpec(memory_space=pltpu....  7.52 us
    ppermute x13, waiting for transfers between devices, sum_over(): parts.append(lax.ppermute(value, axis, pairs))  4.73 us
  transfers between devices with their start and end apart: 49, of which 24 were waited for; matrix products, arithmetic and copies ran while one was open for 0% of the time, Pallas kernels for 5%

profile of v1, /device:TPU:0, one launch (start us, length us, event | category | flops | bytes accessed | tf_op | source)
XLA Modules:
  0.0 172.1 jit_solution(10022647921829385292)
XLA Ops:
  1.7 7.5 %shard_map.50 = (bf16[64,256,512]{2,1,0:T(8,128)(2,1)S(1)}, f32[8,32,128]{2,1,0:T(8,128)S(1)}, f32[8,32,128]{2,1,0:T(8,128)S(1)}, f32[16,32,128]{2,1,0:T(8,128)S...) custom-call(s32[256]{0:T(256)S(1)} %reshape.7.cols_ref, ...), custom_call_target="tpu_custom_call" | custom-call | flops 805306368 | bytes 16777216 | tf_op jit(solution)/shard_map/pallas_call | solution.py:149
  9.2 4.1 %collective-permute-start = (f32[16,32,128]{2,1,0:T(8,128)S(1)}, f32[16,32,128]{2,1,0:T(8,128)S(1)}, u32[]{:S(2)}, u32[]{:S(2)}) collective-permute-start(f32[16,32,128]{2,1,0:T(8,128)S(1)} %get-tuple-element.49), channel_id=1, source_target_pairs={{0,16},{4,20},{8,0},{12,4},{24,8},{28,12},{16,24},{20,28},{1,17},{... | collective-permute-start | bytes 786440 | tf_op jit(solution)/shard_map/ppermute | solution.py:564
  15.3 4.3 %collective-permute-done.2.refs_0_ = f32[8,32,128]{2,1,0:T(8,128)S(1)} collective-permute-done((f32[8,32,128]{2,1,0:T(8,128)S(1)}, f32[8,32,128]{2,1,0:T(8,128)S(1)}, u32[]{:S(2)}, u32[]{:S(2)}) %collective-permute-start.2) | collective-permute-done | bytes 131104 | tf_op jit(solution)/shard_map/ppermute | solution.py:570
  23.5 3.1 %collective-permute-done.3.refs_3_ = f32[8,32,128]{2,1,0:T(8,128)S(1)} collective-permute-done((f32[8,32,128]{2,1,0:T(8,128)S(1)}, f32[8,32,128]{2,1,0:T(8,128)S(1)}, u32[]{:S(2)}, u32[]{:S(2)}) %collective-permute-start.3) | collective-permute-done | bytes 131104 | tf_op jit(solution)/shard_map/ppermute | solution.py:564
  26.6 2.5 %collective-permute-done.5.refs_4_ = f32[8,32,128]{2,1,0:T(8,128)S(1)} collective-permute-done((f32[8,32,128]{2,1,0:T(8,128)S(1)}, f32[8,32,128]{2,1,0:T(8,128)S(1)}, u32[]{:S(2)}, u32[]{:S(2)}) %collective-permute-start.5) | collective-permute-done | bytes 131104 | tf_op jit(solution)/shard_map/ppermute | solution.py:564
  30.8 4.2 %collective-permute-done.7.refs_2_ = f32[8,32,128]{2,1,0:T(8,128)S(1)} collective-permute-done((f32[8,32,128]{2,1,0:T(8,128)S(1)}, f32[8,32,128]{2,1,0:T(8,128)S(1)}, u32[]{:S(2)}, u32[]{:S(2)}) %collective-permute-start.7) | collective-permute-done | bytes 131104 | tf_op jit(solution)/shard_map/ppermute | solution.py:564
  36.5 4.4 %collective-permute-done.9.refs_2_.refs_4_ = f32[8,32,128]{2,1,0:T(8,128)S(1)} collective-permute-done((f32[8,32,128]{2,1,0:T(8,128)S(1)}, f32[8,32,128]{2,1,0:T(8,128)S(1)}, u32[]{:S(2)}, u32[]{:S(2)}) %collective-permute-start.9) | collective-permute-done | bytes 131104 | tf_op jit(solution)/shard_map/ppermute | solution.py:564
  41.0 2.1 %collective-permute-start.11 = (f32[16,32,128]{2,1,0:T(8,128)S(1)}, f32[16,32,128]{2,1,0:T(8,128)S(1)}, u32[]{:S(2)}, u32[]{:S(2)}) collective-permute-start(f32[16,32,128]{2,1,0:T(8,128)S(1)} %shard_map.55), channel_id=1, source_target_pairs={{0,16},{4,20},{8,0},{12,4},{24,8},{28,12},{16,24},{20,28},{1,17},{... | collective-permute-start | bytes 786440 | tf_op jit(solution)/shard_map/ppermute | solution.py:564
  44.5 3.5 %collective-permute-done.10.refs_5_ = f32[8,32,128]{2,1,0:T(8,128)S(1)} collective-permute-done((f32[8,32,128]{2,1,0:T(8,128)S(1)}, f32[8,32,128]{2,1,0:T(8,128)S(1)}, u32[]{:S(2)}, u32[]{:S(2)}) %collective-permute-start.10) | collective-permute-done | bytes 131104 | tf_op jit(solution)/shard_map/ppermute | solution.py:570
  48.2 9.8 %shard_map.56 = (f32[32,8192]{1,0:T(8,128)S(1)}, f32[9,32,128]{2,1,0:T(8,128)S(1)}, f32[9,32,128]{2,1,0:T(8,128)S(1)}, f32[18,32,128]{2,1,0:T(8,128)S(1)}, f32[9...) custom-call(s32[256]{0:T(256)S(1)} %reshape.7.cols_ref, ...), custom_call_target="tpu_custom_call" | custom-call | flops 1610612736 | bytes 8388608 | tf_op jit(solution)/shard_map/pallas_call | solution.py:270
  58.1 2.1 %collective-permute-start.12 = (f32[18,32,128]{2,1,0:T(8,128)S(1)}, f32[18,32,128]{2,1,0:T(8,128)S(1)}, u32[]{:S(2)}, u32[]{:S(2)}) collective-permute-start(f32[18,32,128]{2,1,0:T(8,128)S(1)} %get-tuple-element.56), channel_id=1, source_target_pairs={{0,16},{4,20},{8,0},{12,4},{24,8},{28,12},{16,24},{20,28},{1,17},{... | collective-permute-start | bytes 884744 | tf_op jit(solution)/shard_map/ppermute | solution.py:564
  62.2 4.2 %collective-permute-done.14.refs_0_ = f32[9,32,128]{2,1,0:T(8,128)S(1)} collective-permute-done((f32[9,32,128]{2,1,0:T(8,128)S(1)}, f32[9,32,128]{2,1,0:T(8,128)S(1)}, u32[]{:S(2)}, u32[]{:S(2)}) %collective-permute-start.14) | collective-permute-done | bytes 147488 | tf_op jit(solution)/shard_map/ppermute | solution.py:570
  66.4 2.9 %collective-permute-start.15 = (f32[9,32,128]{2,1,0:T(8,128)S(1)}, f32[9,32,128]{2,1,0:T(8,128)S(1)}, u32[]{:S(2)}, u32[]{:S(2)}) collective-permute-start(f32[9,32,128]{2,1,0:T(8,128)S(1)} %shard_map.58), channel_id=1, source_target_pairs={{0,24},{4,28},{8,16},{12,20},{24,0},{28,4},{16,8},{20,12},{1,25},{... | collective-permute-start | bytes 442376 | tf_op jit(solution)/shard_map/ppermute | solution.py:564
  71.0 2.8 %collective-permute-done.15.refs_3_ = f32[9,32,128]{2,1,0:T(8,128)S(1)} collective-permute-done((f32[9,32,128]{2,1,0:T(8,128)S(1)}, f32[9,32,128]{2,1,0:T(8,128)S(1)}, u32[]{:S(2)}, u32[]{:S(2)}) %collective-permute-start.15) | collective-permute-done | bytes 147488 | tf_op jit(solution)/shard_map/ppermute | solution.py:564
  73.9 3.0 %collective-permute-done.17.refs_4_ = f32[9,32,128]{2,1,0:T(8,128)S(1)} collective-permute-done((f32[9,32,128]{2,1,0:T(8,128)S(1)}, f32[9,32,128]{2,1,0:T(8,128)S(1)}, u32[]{:S(2)}, u32[]{:S(2)}) %collective-permute-start.17) | collective-permute-done | bytes 147488 | tf_op jit(solution)/shard_map/ppermute | solution.py:564
  80.9 1.9 %collective-permute-done.19.refs_2_ = f32[8,32,128]{2,1,0:T(8,128)S(1)} collective-permute-done((f32[8,32,128]{2,1,0:T(8,128)S(1)}, f32[8,32,128]{2,1,0:T(8,128)S(1)}, u32[]{:S(2)}, u32[]{:S(2)}) %collective-permute-start.19) | collective-permute-done | bytes 131104 | tf_op jit(solution)/shard_map/ppermute | solution.py:564
  86.1 2.6 %collective-permute-done.21.refs_2_.refs_4_ = f32[8,32,128]{2,1,0:T(8,128)S(1)} collective-permute-done((f32[8,32,128]{2,1,0:T(8,128)S(1)}, f32[8,32,128]{2,1,0:T(8,128)S(1)}, u32[]{:S(2)}, u32[]{:S(2)}) %collective-permute-start.21) | collective-permute-done | bytes 131104 | tf_op jit(solution)/shard_map/ppermute | solution.py:564
  88.7 2.1 %collective-permute-start.26 = (f32[16,32,128]{2,1,0:T(8,128)S(1)}, f32[16,32,128]{2,1,0:T(8,128)S(1)}, u32[]{:S(2)}, u32[]{:S(2)}) collective-permute-start(f32[16,32,128]{2,1,0:T(8,128)S(1)} %shard_map.62), channel_id=1, source_target_pairs={{0,16},{4,20},{8,0},{12,4},{24,8},{28,12},{16,24},{20,28},{1,17},{... | collective-permute-start | bytes 786440 | tf_op jit(solution)/shard_map/ppermute | solution.py:564
  92.6 3.2 %collective-permute-done.22.refs_5_ = f32[8,32,128]{2,1,0:T(8,128)S(1)} collective-permute-done((f32[8,32,128]{2,1,0:T(8,128)S(1)}, f32[8,32,128]{2,1,0:T(8,128)S(1)}, u32[]{:S(2)}, u32[]{:S(2)}) %collective-permute-start.22) | collective-permute-done | bytes 131104 | tf_op jit(solution)/shard_map/ppermute | solution.py:570
  95.8 11.2 %shard_map.63 = (f32[32,8192]{1,0:T(8,128)S(1)}, f32[32,8192]{1,0:T(8,128)S(1)}, f32[9,32,128]{2,1,0:T(8,128)S(1)}, f32[9,32,128]{2,1,0:T(8,128)S(1)}, f32[18,32...) custom-call(s32[256]{0:T(256)S(1)} %reshape.7.cols_ref, ...), custom_call_target="tpu_custom_call" | custom-call | flops 1610612736 | bytes 8388608 | tf_op jit(solution)/shard_map/pallas_call | solution.py:270
  107.0 2.3 %collective-permute-start.27 = (f32[18,32,128]{2,1,0:T(8,128)S(1)}, f32[18,32,128]{2,1,0:T(8,128)S(1)}, u32[]{:S(2)}, u32[]{:S(2)}) collective-permute-start(f32[18,32,128]{2,1,0:T(8,128)S(1)} %get-tuple-element.68), channel_id=1, source_target_pairs={{0,16},{4,20},{8,0},{12,4},{24,8},{28,12},{16,24},{20,28},{1,17},{... | collective-permute-start | bytes 884744 | tf_op jit(solution)/shard_map/ppermute | solution.py:564
  111.3 3.1 %collective-permute-done.29.refs_0_ = f32[9,32,128]{2,1,0:T(8,128)S(1)} collective-permute-done((f32[9,32,128]{2,1,0:T(8,128)S(1)}, f32[9,32,128]{2,1,0:T(8,128)S(1)}, u32[]{:S(2)}, u32[]{:S(2)}) %collective-permute-start.29) | collective-permute-done | bytes 147488 | tf_op jit(solution)/shard_map/ppermute | solution.py:570
  114.5 2.7 %collective-permute-start.30 = (f32[9,32,128]{2,1,0:T(8,128)S(1)}, f32[9,32,128]{2,1,0:T(8,128)S(1)}, u32[]{:S(2)}, u32[]{:S(2)}) collective-permute-start(f32[9,32,128]{2,1,0:T(8,128)S(1)} %shard_map.65), channel_id=1, source_target_pairs={{0,24},{4,28},{8,16},{12,20},{24,0},{28,4},{16,8},{20,12},{1,25},{... | collective-permute-start | bytes 442376 | tf_op jit(solution)/shard_map/ppermute | solution.py:564
  118.8 2.8 %collective-permute-done.30.refs_3_ = f32[9,32,128]{2,1,0:T(8,128)S(1)} collective-permute-done((f32[9,32,128]{2,1,0:T(8,128)S(1)}, f32[9,32,128]{2,1,0:T(8,128)S(1)}, u32[]{:S(2)}, u32[]{:S(2)}) %collective-permute-start.30) | collective-permute-done | bytes 147488 | tf_op jit(solution)/shard_map/ppermute | solution.py:564
  121.6 3.6 %collective-permute-done.32.refs_4_ = f32[9,32,128]{2,1,0:T(8,128)S(1)} collective-permute-done((f32[9,32,128]{2,1,0:T(8,128)S(1)}, f32[9,32,128]{2,1,0:T(8,128)S(1)}, u32[]{:S(2)}, u32[]{:S(2)}) %collective-permute-start.32) | collective-permute-done | bytes 147488 | tf_op jit(solution)/shard_map/ppermute | solution.py:564
  132.8 2.6 %shard_map.69 = (f32[32,32]{1,0:T(8,128)S(1)}, f32[32,32]{1,0:T(8,128)S(1)}, f32[32,32]{1,0:T(8,128)S(1)}, f32[32,32]{1,0:T(8,128)S(1)}, f32[32,32]{1,0:T(8,128)S(1)}, /*index=5*/f32[32,32]{1,0:T(8,128)S(1)}) custom-call(f32[32,128]{1,0:T(8,128)S(1)} %get-tuple-element.75.refs_0_, f32[32,128]{1,0:T(8,128)S(1)} %collective-permute-done.39.refs_1_, ...), custom_call_target="tpu_custom_call" | custom-call | flops 4000000000 | bytes 4194304 | tf_op jit(solution)/shard_map/pallas_call | solution.py:366
  137.2 2.1 %collective-permute-start.38 = (f32[16,32,128]{2,1,0:T(8,128)S(1)}, f32[16,32,128]{2,1,0:T(8,128)S(1)}, u32[]{:S(2)}, u32[]{:S(2)}) collective-permute-start(f32[16,32,128]{2,1,0:T(8,128)S(1)} %shard_map.68), channel_id=1, source_target_pairs={{0,16},{4,20},{8,0},{12,4},{24,8},{28,12},{16,24},{20,28},{1,17},{... | collective-permute-start | bytes 786440 | tf_op jit(solution)/shard_map/ppermute | solution.py:564
  140.7 2.0 %shard_map.71 = (f32[32,8192]{1,0:T(8,128)S(1)}, f32[32,8192]{1,0:T(8,128)S(1)}) custom-call(f32[32,8192]{1,0:T(8,128)S(1)} %get-tuple-element.66.refs_8_.refs_10_.y0_ref, f32[32,8192]{1,0:T(8,128)S(1)} %get-tuple-element.80.y1_ref, f32[32,8192]{1,0:T(8,128)S(1)} %get-tuple-element.81.u0_ref, f32[32,32]{1,0:T(8,128)S(1)} %get-tuple-element.79.mix_ref, ...), custom_call_target="tpu_custom_call" | custom-call | flops 3000000000 | bytes 4194304 | tf_op jit(solution)/shard_map/pallas_call | solution.py:430
  144.3 8.3 %shard_map.72 = (f32[32,8192]{1,0:T(8,128)S(1)}, f32[32,128]{1,0:T(8,128)S(1)}) custom-call(s32[256]{0:T(256)S(1)} %reshape.7.cols_ref, bf16[64,256,512]{2,1,0:T(8,128)(2,1)S(1)} %get-tuple-element.47.weights_ref, f32[8,32,128]{2,1,0:T(8,128)S(1)} %get-tuple-element.74.refs_0_.p0_ref, f32[8,32,128]{2,1,0:T(8,128)S(1)} %collective-permute-done.33.refs_1_, ...), custom_call_target="tpu_custom_call" | custom-call | flops 805306368 | bytes 8388608 | tf_op jit(solution)/shard_map/pallas_call | solution.py:270
  156.5 1.9 %collective-permute-start.47 = (f32[32,128]{1,0:T(8,128)S(1)}, f32[32,128]{1,0:T(8,128)S(1)}, u32[]{:S(2)}, u32[]{:S(2)}) collective-permute-start(f32[32,128]{1,0:T(8,128)S(1)} %shard_map.73.refs_0_), channel_id=1, source_target_pairs={{0,24},{4,28},{8,16},{12,20},{16,8},{20,12},{24,0},{28,4},{1,25},{... | collective-permute-start | bytes 49160 | tf_op jit(solution)/shard_map/ppermute | solution.py:650
  165.4 1.8 %collective-permute-done.48.refs_1_ = f32[32,128]{1,0:T(8,128)S(1)} collective-permute-done((f32[32,128]{1,0:T(8,128)S(1)}, f32[32,128]{1,0:T(8,128)S(1)}, u32[]{:S(2)}, u32[]{:S(2)}) %collective-permute-start.48) | collective-permute-done | bytes 16416 | tf_op jit(solution)/shard_map/ppermute | solution.py:650
  167.3 4.7 %shard_map.77 = (f32[32,1024]{1,0:T(8,128)}, f32[32,8192]{1,0:T(8,128)}) custom-call(f32[32,128]{1,0:T(8,128)S(1)} %shard_map.74.refs_0_, f32[32,128]{1,0:T(8,128)S(1)} %collective-permute-done.48.refs_1_, f32[32,32]{1,0:T(8,128)S(1)} %get-tuple-element.87.refs_2_, f32[32,32]{1,0:T(8,128)S(1)} %get-tuple-element.88.refs_3_, ...), custom_call_target="tpu_custom_call" | custom-call | tf_op jit(solution)/shard_map/pallas_call | solution.py:485
  (100 shorter events, 51.6 us)
Async XLA Ops:
  9.2 12.8 %collective-permute-start = (f32[16,32,128]{2,1,0:T(8,128)S(1)}, f32[16,32,128]{2,1,0:T(8,128)S(1)}, u32[]{:S(2)}, u32[]{:S(2)}) collective-permute-start(f32[16,32,128]{2,1,0:T(8,128)S(1)} %get-tuple-element.49), channel_id=1, source_target_pairs={{0,16},{4,20},{8,0},{12,4},{24,8},{28,12},{16,24},{20,28},{1,17},{... | collective-permute-start | bytes 786440 | tf_op jit(solution)/shard_map/ppermute | solution.py:564
  13.3 6.4 %collective-permute-start.2 = (f32[8,32,128]{2,1,0:T(8,128)S(1)}, f32[8,32,128]{2,1,0:T(8,128)S(1)}, u32[]{:S(2)}, u32[]{:S(2)}) collective-permute-start(f32[8,32,128]{2,1,0:T(8,128)S(1)} %get-tuple-element.51), channel_id=1, source_target_pairs={{0,4},{4,0},{8,12},{12,8},{24,28},{28,24},{16,20},{20,16},{1,5},{5... | collective-permute-start | bytes 393224 | tf_op jit(solution)/shard_map/ppermute | solution.py:570
  14.8 6.3 %collective-permute-start.4 = (f32[8,32,128]{2,1,0:T(8,128)S(1)}, f32[8,32,128]{2,1,0:T(8,128)S(1)}, u32[]{:S(2)}, u32[]{:S(2)}) collective-permute-start(f32[8,32,128]{2,1,0:T(8,128)S(1)} %get-tuple-element.53), channel_id=1, source_target_pairs={{0,4},{4,0},{8,12},{12,8},{24,28},{28,24},{16,20},{20,16},{1,5},{5... | collective-permute-start | bytes 393224 | tf_op jit(solution)/shard_map/ppermute | solution.py:570
  19.7 6.9 %collective-permute-start.3 = (f32[8,32,128]{2,1,0:T(8,128)S(1)}, f32[8,32,128]{2,1,0:T(8,128)S(1)}, u32[]{:S(2)}, u32[]{:S(2)}) collective-permute-start(f32[8,32,128]{2,1,0:T(8,128)S(1)} %shard_map.52), channel_id=1, source_target_pairs={{0,24},{4,28},{8,16},{12,20},{24,0},{28,4},{16,8},{20,12},{1,25},{... | collective-permute-start | bytes 393224 | tf_op jit(solution)/shard_map/ppermute | solution.py:564
  21.1 8.0 %collective-permute-start.5 = (f32[8,32,128]{2,1,0:T(8,128)S(1)}, f32[8,32,128]{2,1,0:T(8,128)S(1)}, u32[]{:S(2)}, u32[]{:S(2)}) collective-permute-start(f32[8,32,128]{2,1,0:T(8,128)S(1)} %shard_map.53), channel_id=1, source_target_pairs={{0,8},{4,12},{8,24},{12,28},{24,16},{28,20},{16,0},{20,4},{1,9},{5... | collective-permute-start | bytes 393224 | tf_op jit(solution)/shard_map/ppermute | solution.py:564
  22.0 7.1 %collective-permute-start.1 = (f32[8,32,128]{2,1,0:T(8,128)S(1)}, f32[8,32,128]{2,1,0:T(8,128)S(1)}, u32[]{:S(2)}, u32[]{:S(2)}) collective-permute-start(f32[8,32,128]{2,1,0:T(8,128)S(1)} %shard_map.51), channel_id=1, source_target_pairs={{0,4},{4,0},{8,12},{12,8},{24,28},{28,24},{16,20},{20,16},{1,5},{5... | collective-permute-start | bytes 393224 | tf_op jit(solution)/shard_map/ppermute | solution.py:570
  29.1 5.9 %collective-permute-start.7 = (f32[8,32,128]{2,1,0:T(8,128)S(1)}, f32[8,32,128]{2,1,0:T(8,128)S(1)}, u32[]{:S(2)}, u32[]{:S(2)}) collective-permute-start(f32[8,32,128]{2,1,0:T(8,128)S(1)} %shard_map.54.refs_0_.refs_7_.g0_ref), channel_id=1, source_target_pairs={{0,8},{4,12},{8,24},{12,28},{24,16},{28,20},{16,0},{20,4},{1,9},{5... | collective-permute-start | bytes 393224 | tf_op jit(solution)/shard_map/ppermute | solution.py:564
  29.3 7.2 %collective-permute-start.6 = (f32[8,32,128]{2,1,0:T(8,128)S(1)}, f32[8,32,128]{2,1,0:T(8,128)S(1)}, u32[]{:S(2)}, u32[]{:S(2)}) collective-permute-start(f32[8,32,128]{2,1,0:T(8,128)S(1)} %shard_map.54.refs_0_.refs_7_.g0_ref), channel_id=1, source_target_pairs={{0,4},{4,0},{8,12},{12,8},{24,28},{28,24},{16,20},{20,16},{1,5},{5... | collective-permute-start | bytes 393224 | tf_op jit(solution)/shard_map/ppermute | solution.py:570
  35.0 5.9 %collective-permute-start.9 = (f32[8,32,128]{2,1,0:T(8,128)S(1)}, f32[8,32,128]{2,1,0:T(8,128)S(1)}, u32[]{:S(2)}, u32[]{:S(2)}) collective-permute-start(f32[8,32,128]{2,1,0:T(8,128)S(1)} %collective-permute-done.7.refs_2_), channel_id=1, source_target_pairs={{0,8},{4,12},{8,24},{12,28},{24,16},{28,20},{16,0},{20,4},{1,9},{5... | collective-permute-start | bytes 393224 | tf_op jit(solution)/shard_map/ppermute | solution.py:564
  35.0 5.9 %collective-permute-start.8 = (f32[8,32,128]{2,1,0:T(8,128)S(1)}, f32[8,32,128]{2,1,0:T(8,128)S(1)}, u32[]{:S(2)}, u32[]{:S(2)}) collective-permute-start(f32[8,32,128]{2,1,0:T(8,128)S(1)} %collective-permute-done.7.refs_2_), channel_id=1, source_target_pairs={{0,4},{4,0},{8,12},{12,8},{24,28},{28,24},{16,20},{20,16},{1,5},{5... | collective-permute-start | bytes 393224 | tf_op jit(solution)/shard_map/ppermute | solution.py:570
  41.0 7.3 %collective-permute-start.11 = (f32[16,32,128]{2,1,0:T(8,128)S(1)}, f32[16,32,128]{2,1,0:T(8,128)S(1)}, u32[]{:S(2)}, u32[]{:S(2)}) collective-permute-start(f32[16,32,128]{2,1,0:T(8,128)S(1)} %shard_map.55), channel_id=1, source_target_pairs={{0,16},{4,20},{8,0},{12,4},{24,8},{28,12},{16,24},{20,28},{1,17},{... | collective-permute-start | bytes 786440 | tf_op jit(solution)/shard_map/ppermute | solution.py:564
  58.1 11.4 %collective-permute-start.12 = (f32[18,32,128]{2,1,0:T(8,128)S(1)}, f32[18,32,128]{2,1,0:T(8,128)S(1)}, u32[]{:S(2)}, u32[]{:S(2)}) collective-permute-start(f32[18,32,128]{2,1,0:T(8,128)S(1)} %get-tuple-element.56), channel_id=1, source_target_pairs={{0,16},{4,20},{8,0},{12,4},{24,8},{28,12},{16,24},{20,28},{1,17},{... | collective-permute-start | bytes 884744 | tf_op jit(solution)/shard_map/ppermute | solution.py:564
  60.2 6.2 %collective-permute-start.14 = (f32[9,32,128]{2,1,0:T(8,128)S(1)}, f32[9,32,128]{2,1,0:T(8,128)S(1)}, u32[]{:S(2)}, u32[]{:S(2)}) collective-permute-start(f32[9,32,128]{2,1,0:T(8,128)S(1)} %get-tuple-element.58), channel_id=1, source_target_pairs={{0,4},{4,0},{8,12},{12,8},{24,28},{28,24},{16,20},{20,16},{1,5},{5... | collective-permute-start | bytes 442376 | tf_op jit(solution)/shard_map/ppermute | solution.py:570
  61.7 7.7 %collective-permute-start.16 = (f32[9,32,128]{2,1,0:T(8,128)S(1)}, f32[9,32,128]{2,1,0:T(8,128)S(1)}, u32[]{:S(2)}, u32[]{:S(2)}) collective-permute-start(f32[9,32,128]{2,1,0:T(8,128)S(1)} %get-tuple-element.60), channel_id=1, source_target_pairs={{0,4},{4,0},{8,12},{12,8},{24,28},{28,24},{16,20},{20,16},{1,5},{5... | collective-permute-start | bytes 442376 | tf_op jit(solution)/shard_map/ppermute | solution.py:570
  66.4 7.4 %collective-permute-start.15 = (f32[9,32,128]{2,1,0:T(8,128)S(1)}, f32[9,32,128]{2,1,0:T(8,128)S(1)}, u32[]{:S(2)}, u32[]{:S(2)}) collective-permute-start(f32[9,32,128]{2,1,0:T(8,128)S(1)} %shard_map.58), channel_id=1, source_target_pairs={{0,24},{4,28},{8,16},{12,20},{24,0},{28,4},{16,8},{20,12},{1,25},{... | collective-permute-start | bytes 442376 | tf_op jit(solution)/shard_map/ppermute | solution.py:564
  69.4 7.5 %collective-permute-start.17 = (f32[9,32,128]{2,1,0:T(8,128)S(1)}, f32[9,32,128]{2,1,0:T(8,128)S(1)}, u32[]{:S(2)}, u32[]{:S(2)}) collective-permute-start(f32[9,32,128]{2,1,0:T(8,128)S(1)} %shard_map.59), channel_id=1, source_target_pairs={{0,8},{4,12},{8,24},{12,28},{24,16},{28,20},{16,0},{20,4},{1,9},{5... | collective-permute-start | bytes 442376 | tf_op jit(solution)/shard_map/ppermute | solution.py:564
  69.5 7.4 %collective-permute-start.13 = (f32[9,32,128]{2,1,0:T(8,128)S(1)}, f32[9,32,128]{2,1,0:T(8,128)S(1)}, u32[]{:S(2)}, u32[]{:S(2)}) collective-permute-start(f32[9,32,128]{2,1,0:T(8,128)S(1)} %shard_map.57), channel_id=1, source_target_pairs={{0,4},{4,0},{8,12},{12,8},{24,28},{28,24},{16,20},{20,16},{1,5},{5... | collective-permute-start | bytes 442376 | tf_op jit(solution)/shard_map/ppermute | solution.py:570
  76.9 5.9 %collective-permute-start.19 = (f32[8,32,128]{2,1,0:T(8,128)S(1)}, f32[8,32,128]{2,1,0:T(8,128)S(1)}, u32[]{:S(2)}, u32[]{:S(2)}) collective-permute-start(f32[8,32,128]{2,1,0:T(8,128)S(1)} %get-tuple-element.62.refs_0_.q0_ref), channel_id=1, source_target_pairs={{0,8},{4,12},{8,24},{12,28},{24,16},{28,20},{16,0},{20,4},{1,9},{5... | collective-permute-start | bytes 393224 | tf_op jit(solution)/shard_map/ppermute | solution.py:564
  77.6 5.9 %collective-permute-start.25 = (f32[32,128]{1,0:T(8,128)S(1)}, f32[32,128]{1,0:T(8,128)S(1)}, u32[]{:S(2)}, u32[]{:S(2)}) collective-permute-start(f32[32,128]{1,0:T(8,128)S(1)} %get-tuple-element.63.refs_0_), channel_id=1, source_target_pairs={{0,3},{1,2},{2,1},{3,0},{4,7},{5,6},{6,5},{7,4},{8,11},{9,10},{10,... | collective-permute-start | bytes 49160 | tf_op jit(solution)/shard_map/ppermute | solution.py:650
  77.6 6.8 %collective-permute-start.24 = (f32[32,128]{1,0:T(8,128)S(1)}, f32[32,128]{1,0:T(8,128)S(1)}, u32[]{:S(2)}, u32[]{:S(2)}) collective-permute-start(f32[32,128]{1,0:T(8,128)S(1)} %get-tuple-element.63.refs_0_), channel_id=1, source_target_pairs={{0,2},{1,3},{2,0},{3,1},{4,6},{5,7},{6,4},{7,5},{8,10},{9,11},{10,... | collective-permute-start | bytes 49160 | tf_op jit(solution)/shard_map/ppermute | solution.py:650
  79.4 6.6 %collective-permute-start.18 = (f32[8,32,128]{2,1,0:T(8,128)S(1)}, f32[8,32,128]{2,1,0:T(8,128)S(1)}, u32[]{:S(2)}, u32[]{:S(2)}) collective-permute-start(f32[8,32,128]{2,1,0:T(8,128)S(1)} %get-tuple-element.62.refs_0_.q0_ref), channel_id=1, source_target_pairs={{0,4},{4,0},{8,12},{12,8},{24,28},{28,24},{16,20},{20,16},{1,5},{5... | collective-permute-start | bytes 393224 | tf_op jit(solution)/shard_map/ppermute | solution.py:570
  88.7 7.0 %collective-permute-start.26 = (f32[16,32,128]{2,1,0:T(8,128)S(1)}, f32[16,32,128]{2,1,0:T(8,128)S(1)}, u32[]{:S(2)}, u32[]{:S(2)}) collective-permute-start(f32[16,32,128]{2,1,0:T(8,128)S(1)} %shard_map.62), channel_id=1, source_target_pairs={{0,16},{4,20},{8,0},{12,4},{24,8},{28,12},{16,24},{20,28},{1,17},{... | collective-permute-start | bytes 786440 | tf_op jit(solution)/shard_map/ppermute | solution.py:564
  107.0 10.3 %collective-permute-start.27 = (f32[18,32,128]{2,1,0:T(8,128)S(1)}, f32[18,32,128]{2,1,0:T(8,128)S(1)}, u32[]{:S(2)}, u32[]{:S(2)}) collective-permute-start(f32[18,32,128]{2,1,0:T(8,128)S(1)} %get-tuple-element.68), channel_id=1, source_target_pairs={{0,16},{4,20},{8,0},{12,4},{24,8},{28,12},{16,24},{20,28},{1,17},{... | collective-permute-start | bytes 884744 | tf_op jit(solution)/shard_map/ppermute | solution.py:564
  110.8 6.3 %collective-permute-start.31 = (f32[9,32,128]{2,1,0:T(8,128)S(1)}, f32[9,32,128]{2,1,0:T(8,128)S(1)}, u32[]{:S(2)}, u32[]{:S(2)}) collective-permute-start(f32[9,32,128]{2,1,0:T(8,128)S(1)} %get-tuple-element.72), channel_id=1, source_target_pairs={{0,4},{4,0},{8,12},{12,8},{24,28},{28,24},{16,20},{20,16},{1,5},{5... | collective-permute-start | bytes 442376 | tf_op jit(solution)/shard_map/ppermute | solution.py:570
  114.5 7.1 %collective-permute-start.30 = (f32[9,32,128]{2,1,0:T(8,128)S(1)}, f32[9,32,128]{2,1,0:T(8,128)S(1)}, u32[]{:S(2)}, u32[]{:S(2)}) collective-permute-start(f32[9,32,128]{2,1,0:T(8,128)S(1)} %shard_map.65), channel_id=1, source_target_pairs={{0,24},{4,28},{8,16},{12,20},{24,0},{28,4},{16,8},{20,12},{1,25},{... | collective-permute-start | bytes 442376 | tf_op jit(solution)/shard_map/ppermute | solution.py:564
  117.2 8.0 %collective-permute-start.32 = (f32[9,32,128]{2,1,0:T(8,128)S(1)}, f32[9,32,128]{2,1,0:T(8,128)S(1)}, u32[]{:S(2)}, u32[]{:S(2)}) collective-permute-start(f32[9,32,128]{2,1,0:T(8,128)S(1)} %shard_map.66), channel_id=1, source_target_pairs={{0,8},{4,12},{8,24},{12,28},{24,16},{28,20},{16,0},{20,4},{1,9},{5... | collective-permute-start | bytes 442376 | tf_op jit(solution)/shard_map/ppermute | solution.py:564
  117.3 7.9 %collective-permute-start.28 = (f32[9,32,128]{2,1,0:T(8,128)S(1)}, f32[9,32,128]{2,1,0:T(8,128)S(1)}, u32[]{:S(2)}, u32[]{:S(2)}) collective-permute-start(f32[9,32,128]{2,1,0:T(8,128)S(1)} %shard_map.64), channel_id=1, source_target_pairs={{0,4},{4,0},{8,12},{12,8},{24,28},{28,24},{16,20},{20,16},{1,5},{5... | collective-permute-start | bytes 442376 | tf_op jit(solution)/shard_map/ppermute | solution.py:570
  125.2 6.1 %collective-permute-start.34 = (f32[8,32,128]{2,1,0:T(8,128)S(1)}, f32[8,32,128]{2,1,0:T(8,128)S(1)}, u32[]{:S(2)}, u32[]{:S(2)}) collective-permute-start(f32[8,32,128]{2,1,0:T(8,128)S(1)} %get-tuple-element.74.refs_0_.p0_ref), channel_id=1, source_target_pairs={{0,8},{4,12},{8,24},{12,28},{24,16},{28,20},{16,0},{20,4},{1,9},{5... | collective-permute-start | bytes 393224 | tf_op jit(solution)/shard_map/ppermute | solution.py:564
  126.2 6.6 %collective-permute-start.40 = (f32[32,128]{1,0:T(8,128)S(1)}, f32[32,128]{1,0:T(8,128)S(1)}, u32[]{:S(2)}, u32[]{:S(2)}) collective-permute-start(f32[32,128]{1,0:T(8,128)S(1)} %get-tuple-element.75.refs_0_), channel_id=1, source_target_pairs={{0,2},{1,3},{2,0},{3,1},{4,6},{5,7},{6,4},{7,5},{8,10},{9,11},{10,... | collective-permute-start | bytes 49160 | tf_op jit(solution)/shard_map/ppermute | solution.py:650
  128.1 7.3 %collective-permute-start.33 = (f32[8,32,128]{2,1,0:T(8,128)S(1)}, f32[8,32,128]{2,1,0:T(8,128)S(1)}, u32[]{:S(2)}, u32[]{:S(2)}) collective-permute-start(f32[8,32,128]{2,1,0:T(8,128)S(1)} %get-tuple-element.74.refs_0_.p0_ref), channel_id=1, source_target_pairs={{0,4},{4,0},{8,12},{12,8},{24,28},{28,24},{16,20},{20,16},{1,5},{5... | collective-permute-start | bytes 393224 | tf_op jit(solution)/shard_map/ppermute | solution.py:570
  137.2 7.0 %collective-permute-start.38 = (f32[16,32,128]{2,1,0:T(8,128)S(1)}, f32[16,32,128]{2,1,0:T(8,128)S(1)}, u32[]{:S(2)}, u32[]{:S(2)}) collective-permute-start(f32[16,32,128]{2,1,0:T(8,128)S(1)} %shard_map.68), channel_id=1, source_target_pairs={{0,16},{4,20},{8,0},{12,4},{24,8},{28,12},{16,24},{20,28},{1,17},{... | collective-permute-start | bytes 786440 | tf_op jit(solution)/shard_map/ppermute | solution.py:564
  156.5 6.1 %collective-permute-start.47 = (f32[32,128]{1,0:T(8,128)S(1)}, f32[32,128]{1,0:T(8,128)S(1)}, u32[]{:S(2)}, u32[]{:S(2)}) collective-permute-start(f32[32,128]{1,0:T(8,128)S(1)} %shard_map.73.refs_0_), channel_id=1, source_target_pairs={{0,24},{4,28},{8,16},{12,20},{16,8},{20,12},{24,0},{28,4},{1,25},{... | collective-permute-start | bytes 49160 | tf_op jit(solution)/shard_map/ppermute | solution.py:650
  (18 other events, 100.0 us)

commit v2 on v1

--- a/solution.py
+++ b/solution.py
@@ -9,7 +9,7 @@
 
 CBD = 8
 COPY_ROWS = 4
-STEP_ROWS = 16
+STEP_ROWS = 32
 MIB = 1024 * 1024
 F32 = jnp.float32
 BF16 = jnp.bfloat16

time: 172 us -> 170 us (0.988)
  Pallas kernels: 51 us -> 48.7 us
    pallas_call x3, Pallas kernels: 29.3 us -> 27 us  [sweep(): pl.pallas_call(functools.partial(sweep_kernel, len(vectors), len(groups),...]
where the time goes in v2:
time: 170 us
  starting transfers between devices  60.5 us (36%)
  waiting for transfers between devices  58.5 us (34%)
  Pallas kernels  48.7 us (29%)
    ppermute x18, waiting for transfers between devices, next_z(): return lax.ppermute(value, 'row', pairs)  34.4 us
    pallas_call x3, Pallas kernels, sweep(): pl.pallas_call(functools.partial(sweep_kernel, len(vectors), len(groups),...  27 us
    ppermute x18, starting transfers between devices, next_z(): return lax.ppermute(value, 'row', pairs)  25.4 us
    ppermute x18, starting transfers between devices, next_x(): return lax.ppermute(value, 'row', pairs)  23.7 us
    ppermute x18, waiting for transfers between devices, next_x(): return lax.ppermute(value, 'row', pairs)  19.3 us
    ppermute x13, starting transfers between devices, sum_over(): parts.append(lax.ppermute(value, axis, pairs))  11.4 us
    pallas_call x1, Pallas kernels, prepare(): pl.pallas_call(prepare_kernel, in_specs=[pl.BlockSpec(memory_space=pltpu....  7.52 us
    ppermute x13, waiting for transfers between devices, sum_over(): parts.append(lax.ppermute(value, axis, pairs))  4.74 us
  transfers between devices with their start and end apart: 49, of which 24 were waited for; matrix products, arithmetic and copies ran while one was open for 0% of the time, Pallas kernels for 5%

profile of v2, /device:TPU:0, one launch (start us, length us, event | category | flops | bytes accessed | tf_op | source)
XLA Modules:
  0.0 170.0 jit_solution(10042399085523704735)
XLA Ops:
  1.7 7.5 %shard_map.50 = (bf16[64,256,512]{2,1,0:T(8,128)(2,1)S(1)}, f32[8,32,128]{2,1,0:T(8,128)S(1)}, f32[8,32,128]{2,1,0:T(8,128)S(1)}, f32[16,32,128]{2,1,0:T(8,128)S...) custom-call(s32[256]{0:T(256)S(1)} %reshape.7.cols_ref, ...), custom_call_target="tpu_custom_call" | custom-call | flops 805306368 | bytes 16777216 | tf_op jit(solution)/shard_map/pallas_call | solution.py:149
  9.2 4.1 %collective-permute-start = (f32[16,32,128]{2,1,0:T(8,128)S(1)}, f32[16,32,128]{2,1,0:T(8,128)S(1)}, u32[]{:S(2)}, u32[]{:S(2)}) collective-permute-start(f32[16,32,128]{2,1,0:T(8,128)S(1)} %get-tuple-element.49), channel_id=1, source_target_pairs={{0,16},{4,20},{8,0},{12,4},{24,8},{28,12},{16,24},{20,28},{1,17},{... | collective-permute-start | bytes 786440 | tf_op jit(solution)/shard_map/ppermute | solution.py:564
  15.3 4.3 %collective-permute-done.2.refs_0_ = f32[8,32,128]{2,1,0:T(8,128)S(1)} collective-permute-done((f32[8,32,128]{2,1,0:T(8,128)S(1)}, f32[8,32,128]{2,1,0:T(8,128)S(1)}, u32[]{:S(2)}, u32[]{:S(2)}) %collective-permute-start.2) | collective-permute-done | bytes 131104 | tf_op jit(solution)/shard_map/ppermute | solution.py:570
  23.5 3.1 %collective-permute-done.3.refs_3_ = f32[8,32,128]{2,1,0:T(8,128)S(1)} collective-permute-done((f32[8,32,128]{2,1,0:T(8,128)S(1)}, f32[8,32,128]{2,1,0:T(8,128)S(1)}, u32[]{:S(2)}, u32[]{:S(2)}) %collective-permute-start.3) | collective-permute-done | bytes 131104 | tf_op jit(solution)/shard_map/ppermute | solution.py:564
  26.6 2.5 %collective-permute-done.5.refs_4_ = f32[8,32,128]{2,1,0:T(8,128)S(1)} collective-permute-done((f32[8,32,128]{2,1,0:T(8,128)S(1)}, f32[8,32,128]{2,1,0:T(8,128)S(1)}, u32[]{:S(2)}, u32[]{:S(2)}) %collective-permute-start.5) | collective-permute-done | bytes 131104 | tf_op jit(solution)/shard_map/ppermute | solution.py:564
  30.8 4.2 %collective-permute-done.7.refs_2_ = f32[8,32,128]{2,1,0:T(8,128)S(1)} collective-permute-done((f32[8,32,128]{2,1,0:T(8,128)S(1)}, f32[8,32,128]{2,1,0:T(8,128)S(1)}, u32[]{:S(2)}, u32[]{:S(2)}) %collective-permute-start.7) | collective-permute-done | bytes 131104 | tf_op jit(solution)/shard_map/ppermute | solution.py:564
  36.5 4.4 %collective-permute-done.9.refs_2_.refs_4_ = f32[8,32,128]{2,1,0:T(8,128)S(1)} collective-permute-done((f32[8,32,128]{2,1,0:T(8,128)S(1)}, f32[8,32,128]{2,1,0:T(8,128)S(1)}, u32[]{:S(2)}, u32[]{:S(2)}) %collective-permute-start.9) | collective-permute-done | bytes 131104 | tf_op jit(solution)/shard_map/ppermute | solution.py:564
  41.0 2.1 %collective-permute-start.11 = (f32[16,32,128]{2,1,0:T(8,128)S(1)}, f32[16,32,128]{2,1,0:T(8,128)S(1)}, u32[]{:S(2)}, u32[]{:S(2)}) collective-permute-start(f32[16,32,128]{2,1,0:T(8,128)S(1)} %shard_map.55), channel_id=1, source_target_pairs={{0,16},{4,20},{8,0},{12,4},{24,8},{28,12},{16,24},{20,28},{1,17},{... | collective-permute-start | bytes 786440 | tf_op jit(solution)/shard_map/ppermute | solution.py:564
  44.5 3.5 %collective-permute-done.10.refs_5_ = f32[8,32,128]{2,1,0:T(8,128)S(1)} collective-permute-done((f32[8,32,128]{2,1,0:T(8,128)S(1)}, f32[8,32,128]{2,1,0:T(8,128)S(1)}, u32[]{:S(2)}, u32[]{:S(2)}) %collective-permute-start.10) | collective-permute-done | bytes 131104 | tf_op jit(solution)/shard_map/ppermute | solution.py:570
  48.2 9.6 %shard_map.56 = (f32[32,8192]{1,0:T(8,128)S(1)}, f32[9,32,128]{2,1,0:T(8,128)S(1)}, f32[9,32,128]{2,1,0:T(8,128)S(1)}, f32[18,32,128]{2,1,0:T(8,128)S(1)}, f32[9...) custom-call(s32[256]{0:T(256)S(1)} %reshape.7.cols_ref, ...), custom_call_target="tpu_custom_call" | custom-call | flops 1610612736 | bytes 8388608 | tf_op jit(solution)/shard_map/pallas_call | solution.py:270
  57.8 2.1 %collective-permute-start.12 = (f32[18,32,128]{2,1,0:T(8,128)S(1)}, f32[18,32,128]{2,1,0:T(8,128)S(1)}, u32[]{:S(2)}, u32[]{:S(2)}) collective-permute-start(f32[18,32,128]{2,1,0:T(8,128)S(1)} %get-tuple-element.56), channel_id=1, source_target_pairs={{0,16},{4,20},{8,0},{12,4},{24,8},{28,12},{16,24},{20,28},{1,17},{... | collective-permute-start | bytes 884744 | tf_op jit(solution)/shard_map/ppermute | solution.py:564
  62.0 4.2 %collective-permute-done.14.refs_0_ = f32[9,32,128]{2,1,0:T(8,128)S(1)} collective-permute-done((f32[9,32,128]{2,1,0:T(8,128)S(1)}, f32[9,32,128]{2,1,0:T(8,128)S(1)}, u32[]{:S(2)}, u32[]{:S(2)}) %collective-permute-start.14) | collective-permute-done | bytes 147488 | tf_op jit(solution)/shard_map/ppermute | solution.py:570
  66.3 2.8 %collective-permute-start.15 = (f32[9,32,128]{2,1,0:T(8,128)S(1)}, f32[9,32,128]{2,1,0:T(8,128)S(1)}, u32[]{:S(2)}, u32[]{:S(2)}) collective-permute-start(f32[9,32,128]{2,1,0:T(8,128)S(1)} %shard_map.58), channel_id=1, source_target_pairs={{0,24},{4,28},{8,16},{12,20},{24,0},{28,4},{16,8},{20,12},{1,25},{... | collective-permute-start | bytes 442376 | tf_op jit(solution)/shard_map/ppermute | solution.py:564
  70.8 2.8 %collective-permute-done.15.refs_3_ = f32[9,32,128]{2,1,0:T(8,128)S(1)} collective-permute-done((f32[9,32,128]{2,1,0:T(8,128)S(1)}, f32[9,32,128]{2,1,0:T(8,128)S(1)}, u32[]{:S(2)}, u32[]{:S(2)}) %collective-permute-start.15) | collective-permute-done | bytes 147488 | tf_op jit(solution)/shard_map/ppermute | solution.py:564
  73.6 3.0 %collective-permute-done.17.refs_4_ = f32[9,32,128]{2,1,0:T(8,128)S(1)} collective-permute-done((f32[9,32,128]{2,1,0:T(8,128)S(1)}, f32[9,32,128]{2,1,0:T(8,128)S(1)}, u32[]{:S(2)}, u32[]{:S(2)}) %collective-permute-start.17) | collective-permute-done | bytes 147488 | tf_op jit(solution)/shard_map/ppermute | solution.py:564
  80.7 1.9 %collective-permute-done.19.refs_2_ = f32[8,32,128]{2,1,0:T(8,128)S(1)} collective-permute-done((f32[8,32,128]{2,1,0:T(8,128)S(1)}, f32[8,32,128]{2,1,0:T(8,128)S(1)}, u32[]{:S(2)}, u32[]{:S(2)}) %collective-permute-start.19) | collective-permute-done | bytes 131104 | tf_op jit(solution)/shard_map/ppermute | solution.py:564
  85.8 2.7 %collective-permute-done.21.refs_2_.refs_4_ = f32[8,32,128]{2,1,0:T(8,128)S(1)} collective-permute-done((f32[8,32,128]{2,1,0:T(8,128)S(1)}, f32[8,32,128]{2,1,0:T(8,128)S(1)}, u32[]{:S(2)}, u32[]{:S(2)}) %collective-permute-start.21) | collective-permute-done | bytes 131104 | tf_op jit(solution)/shard_map/ppermute | solution.py:564
  88.5 2.3 %collective-permute-start.26 = (f32[16,32,128]{2,1,0:T(8,128)S(1)}, f32[16,32,128]{2,1,0:T(8,128)S(1)}, u32[]{:S(2)}, u32[]{:S(2)}) collective-permute-start(f32[16,32,128]{2,1,0:T(8,128)S(1)} %shard_map.62), channel_id=1, source_target_pairs={{0,16},{4,20},{8,0},{12,4},{24,8},{28,12},{16,24},{20,28},{1,17},{... | collective-permute-start | bytes 786440 | tf_op jit(solution)/shard_map/ppermute | solution.py:564
  92.6 3.2 %collective-permute-done.22.refs_5_ = f32[8,32,128]{2,1,0:T(8,128)S(1)} collective-permute-done((f32[8,32,128]{2,1,0:T(8,128)S(1)}, f32[8,32,128]{2,1,0:T(8,128)S(1)}, u32[]{:S(2)}, u32[]{:S(2)}) %collective-permute-start.22) | collective-permute-done | bytes 131104 | tf_op jit(solution)/shard_map/ppermute | solution.py:570
  95.7 10.0 %shard_map.63 = (f32[32,8192]{1,0:T(8,128)S(1)}, f32[32,8192]{1,0:T(8,128)S(1)}, f32[9,32,128]{2,1,0:T(8,128)S(1)}, f32[9,32,128]{2,1,0:T(8,128)S(1)}, f32[18,32...) custom-call(s32[256]{0:T(256)S(1)} %reshape.7.cols_ref, ...), custom_call_target="tpu_custom_call" | custom-call | flops 1610612736 | bytes 8388608 | tf_op jit(solution)/shard_map/pallas_call | solution.py:270
  105.8 2.4 %collective-permute-start.27 = (f32[18,32,128]{2,1,0:T(8,128)S(1)}, f32[18,32,128]{2,1,0:T(8,128)S(1)}, u32[]{:S(2)}, u32[]{:S(2)}) collective-permute-start(f32[18,32,128]{2,1,0:T(8,128)S(1)} %get-tuple-element.68), channel_id=1, source_target_pairs={{0,16},{4,20},{8,0},{12,4},{24,8},{28,12},{16,24},{20,28},{1,17},{... | collective-permute-start | bytes 884744 | tf_op jit(solution)/shard_map/ppermute | solution.py:564
  110.2 3.1 %collective-permute-done.29.refs_0_ = f32[9,32,128]{2,1,0:T(8,128)S(1)} collective-permute-done((f32[9,32,128]{2,1,0:T(8,128)S(1)}, f32[9,32,128]{2,1,0:T(8,128)S(1)}, u32[]{:S(2)}, u32[]{:S(2)}) %collective-permute-start.29) | collective-permute-done | bytes 147488 | tf_op jit(solution)/shard_map/ppermute | solution.py:570
  113.3 2.6 %collective-permute-start.30 = (f32[9,32,128]{2,1,0:T(8,128)S(1)}, f32[9,32,128]{2,1,0:T(8,128)S(1)}, u32[]{:S(2)}, u32[]{:S(2)}) collective-permute-start(f32[9,32,128]{2,1,0:T(8,128)S(1)} %shard_map.65), channel_id=1, source_target_pairs={{0,24},{4,28},{8,16},{12,20},{24,0},{28,4},{16,8},{20,12},{1,25},{... | collective-permute-start | bytes 442376 | tf_op jit(solution)/shard_map/ppermute | solution.py:564
  117.7 2.7 %collective-permute-done.30.refs_3_ = f32[9,32,128]{2,1,0:T(8,128)S(1)} collective-permute-done((f32[9,32,128]{2,1,0:T(8,128)S(1)}, f32[9,32,128]{2,1,0:T(8,128)S(1)}, u32[]{:S(2)}, u32[]{:S(2)}) %collective-permute-start.30) | collective-permute-done | bytes 147488 | tf_op jit(solution)/shard_map/ppermute | solution.py:564
  120.4 3.6 %collective-permute-done.32.refs_4_ = f32[9,32,128]{2,1,0:T(8,128)S(1)} collective-permute-done((f32[9,32,128]{2,1,0:T(8,128)S(1)}, f32[9,32,128]{2,1,0:T(8,128)S(1)}, u32[]{:S(2)}, u32[]{:S(2)}) %collective-permute-start.32) | collective-permute-done | bytes 147488 | tf_op jit(solution)/shard_map/ppermute | solution.py:564
  131.5 2.6 %shard_map.69 = (f32[32,32]{1,0:T(8,128)S(1)}, f32[32,32]{1,0:T(8,128)S(1)}, f32[32,32]{1,0:T(8,128)S(1)}, f32[32,32]{1,0:T(8,128)S(1)}, f32[32,32]{1,0:T(8,128)S(1)}, /*index=5*/f32[32,32]{1,0:T(8,128)S(1)}) custom-call(f32[32,128]{1,0:T(8,128)S(1)} %get-tuple-element.75.refs_0_, f32[32,128]{1,0:T(8,128)S(1)} %collective-permute-done.39.refs_1_, ...), custom_call_target="tpu_custom_call" | custom-call | flops 4000000000 | bytes 4194304 | tf_op jit(solution)/shard_map/pallas_call | solution.py:366
  135.9 2.3 %collective-permute-start.38 = (f32[16,32,128]{2,1,0:T(8,128)S(1)}, f32[16,32,128]{2,1,0:T(8,128)S(1)}, u32[]{:S(2)}, u32[]{:S(2)}) collective-permute-start(f32[16,32,128]{2,1,0:T(8,128)S(1)} %shard_map.68), channel_id=1, source_target_pairs={{0,16},{4,20},{8,0},{12,4},{24,8},{28,12},{16,24},{20,28},{1,17},{... | collective-permute-start | bytes 786440 | tf_op jit(solution)/shard_map/ppermute | solution.py:564
  139.5 2.0 %shard_map.71 = (f32[32,8192]{1,0:T(8,128)S(1)}, f32[32,8192]{1,0:T(8,128)S(1)}) custom-call(f32[32,8192]{1,0:T(8,128)S(1)} %get-tuple-element.66.refs_8_.refs_10_.y0_ref, f32[32,8192]{1,0:T(8,128)S(1)} %get-tuple-element.80.y1_ref, f32[32,8192]{1,0:T(8,128)S(1)} %get-tuple-element.81.u0_ref, f32[32,32]{1,0:T(8,128)S(1)} %get-tuple-element.79.mix_ref, ...), custom_call_target="tpu_custom_call" | custom-call | flops 3000000000 | bytes 4194304 | tf_op jit(solution)/shard_map/pallas_call | solution.py:430
  143.1 7.3 %shard_map.72 = (f32[32,8192]{1,0:T(8,128)S(1)}, f32[32,128]{1,0:T(8,128)S(1)}) custom-call(s32[256]{0:T(256)S(1)} %reshape.7.cols_ref, bf16[64,256,512]{2,1,0:T(8,128)(2,1)S(1)} %get-tuple-element.47.weights_ref, f32[8,32,128]{2,1,0:T(8,128)S(1)} %get-tuple-element.74.refs_0_.p0_ref, f32[8,32,128]{2,1,0:T(8,128)S(1)} %collective-permute-done.33.refs_1_, ...), custom_call_target="tpu_custom_call" | custom-call | flops 805306368 | bytes 8388608 | tf_op jit(solution)/shard_map/pallas_call | solution.py:270
  154.4 1.9 %collective-permute-start.47 = (f32[32,128]{1,0:T(8,128)S(1)}, f32[32,128]{1,0:T(8,128)S(1)}, u32[]{:S(2)}, u32[]{:S(2)}) collective-permute-start(f32[32,128]{1,0:T(8,128)S(1)} %shard_map.73.refs_0_), channel_id=1, source_target_pairs={{0,24},{4,28},{8,16},{12,20},{16,8},{20,12},{24,0},{28,4},{1,25},{... | collective-permute-start | bytes 49160 | tf_op jit(solution)/shard_map/ppermute | solution.py:650
  163.3 1.8 %collective-permute-done.48.refs_1_ = f32[32,128]{1,0:T(8,128)S(1)} collective-permute-done((f32[32,128]{1,0:T(8,128)S(1)}, f32[32,128]{1,0:T(8,128)S(1)}, u32[]{:S(2)}, u32[]{:S(2)}) %collective-permute-start.48) | collective-permute-done | bytes 16416 | tf_op jit(solution)/shard_map/ppermute | solution.py:650
  165.2 4.7 %shard_map.77 = (f32[32,1024]{1,0:T(8,128)}, f32[32,8192]{1,0:T(8,128)}) custom-call(f32[32,128]{1,0:T(8,128)S(1)} %shard_map.74.refs_0_, f32[32,128]{1,0:T(8,128)S(1)} %collective-permute-done.48.refs_1_, f32[32,32]{1,0:T(8,128)S(1)} %get-tuple-element.87.refs_2_, f32[32,32]{1,0:T(8,128)S(1)} %get-tuple-element.88.refs_3_, ...), custom_call_target="tpu_custom_call" | custom-call | tf_op jit(solution)/shard_map/pallas_call | solution.py:485
  (100 shorter events, 51.6 us)
Async XLA Ops:
  9.2 12.8 %collective-permute-start = (f32[16,32,128]{2,1,0:T(8,128)S(1)}, f32[16,32,128]{2,1,0:T(8,128)S(1)}, u32[]{:S(2)}, u32[]{:S(2)}) collective-permute-start(f32[16,32,128]{2,1,0:T(8,128)S(1)} %get-tuple-element.49), channel_id=1, source_target_pairs={{0,16},{4,20},{8,0},{12,4},{24,8},{28,12},{16,24},{20,28},{1,17},{... | collective-permute-start | bytes 786440 | tf_op jit(solution)/shard_map/ppermute | solution.py:564
  13.3 6.4 %collective-permute-start.2 = (f32[8,32,128]{2,1,0:T(8,128)S(1)}, f32[8,32,128]{2,1,0:T(8,128)S(1)}, u32[]{:S(2)}, u32[]{:S(2)}) collective-permute-start(f32[8,32,128]{2,1,0:T(8,128)S(1)} %get-tuple-element.51), channel_id=1, source_target_pairs={{0,4},{4,0},{8,12},{12,8},{24,28},{28,24},{16,20},{20,16},{1,5},{5... | collective-permute-start | bytes 393224 | tf_op jit(solution)/shard_map/ppermute | solution.py:570
  14.8 6.3 %collective-permute-start.4 = (f32[8,32,128]{2,1,0:T(8,128)S(1)}, f32[8,32,128]{2,1,0:T(8,128)S(1)}, u32[]{:S(2)}, u32[]{:S(2)}) collective-permute-start(f32[8,32,128]{2,1,0:T(8,128)S(1)} %get-tuple-element.53), channel_id=1, source_target_pairs={{0,4},{4,0},{8,12},{12,8},{24,28},{28,24},{16,20},{20,16},{1,5},{5... | collective-permute-start | bytes 393224 | tf_op jit(solution)/shard_map/ppermute | solution.py:570
  19.7 6.9 %collective-permute-start.3 = (f32[8,32,128]{2,1,0:T(8,128)S(1)}, f32[8,32,128]{2,1,0:T(8,128)S(1)}, u32[]{:S(2)}, u32[]{:S(2)}) collective-permute-start(f32[8,32,128]{2,1,0:T(8,128)S(1)} %shard_map.52), channel_id=1, source_target_pairs={{0,24},{4,28},{8,16},{12,20},{24,0},{28,4},{16,8},{20,12},{1,25},{... | collective-permute-start | bytes 393224 | tf_op jit(solution)/shard_map/ppermute | solution.py:564
  21.1 8.0 %collective-permute-start.5 = (f32[8,32,128]{2,1,0:T(8,128)S(1)}, f32[8,32,128]{2,1,0:T(8,128)S(1)}, u32[]{:S(2)}, u32[]{:S(2)}) collective-permute-start(f32[8,32,128]{2,1,0:T(8,128)S(1)} %shard_map.53), channel_id=1, source_target_pairs={{0,8},{4,12},{8,24},{12,28},{24,16},{28,20},{16,0},{20,4},{1,9},{5... | collective-permute-start | bytes 393224 | tf_op jit(solution)/shard_map/ppermute | solution.py:564
  22.0 7.1 %collective-permute-start.1 = (f32[8,32,128]{2,1,0:T(8,128)S(1)}, f32[8,32,128]{2,1,0:T(8,128)S(1)}, u32[]{:S(2)}, u32[]{:S(2)}) collective-permute-start(f32[8,32,128]{2,1,0:T(8,128)S(1)} %shard_map.51), channel_id=1, source_target_pairs={{0,4},{4,0},{8,12},{12,8},{24,28},{28,24},{16,20},{20,16},{1,5},{5... | collective-permute-start | bytes 393224 | tf_op jit(solution)/shard_map/ppermute | solution.py:570
  29.1 5.9 %collective-permute-start.7 = (f32[8,32,128]{2,1,0:T(8,128)S(1)}, f32[8,32,128]{2,1,0:T(8,128)S(1)}, u32[]{:S(2)}, u32[]{:S(2)}) collective-permute-start(f32[8,32,128]{2,1,0:T(8,128)S(1)} %shard_map.54.refs_0_.refs_7_.g0_ref), channel_id=1, source_target_pairs={{0,8},{4,12},{8,24},{12,28},{24,16},{28,20},{16,0},{20,4},{1,9},{5... | collective-permute-start | bytes 393224 | tf_op jit(solution)/shard_map/ppermute | solution.py:564
  29.3 7.2 %collective-permute-start.6 = (f32[8,32,128]{2,1,0:T(8,128)S(1)}, f32[8,32,128]{2,1,0:T(8,128)S(1)}, u32[]{:S(2)}, u32[]{:S(2)}) collective-permute-start(f32[8,32,128]{2,1,0:T(8,128)S(1)} %shard_map.54.refs_0_.refs_7_.g0_ref), channel_id=1, source_target_pairs={{0,4},{4,0},{8,12},{12,8},{24,28},{28,24},{16,20},{20,16},{1,5},{5... | collective-permute-start | bytes 393224 | tf_op jit(solution)/shard_map/ppermute | solution.py:570
  35.0 5.9 %collective-permute-start.9 = (f32[8,32,128]{2,1,0:T(8,128)S(1)}, f32[8,32,128]{2,1,0:T(8,128)S(1)}, u32[]{:S(2)}, u32[]{:S(2)}) collective-permute-start(f32[8,32,128]{2,1,0:T(8,128)S(1)} %collective-permute-done.7.refs_2_), channel_id=1, source_target_pairs={{0,8},{4,12},{8,24},{12,28},{24,16},{28,20},{16,0},{20,4},{1,9},{5... | collective-permute-start | bytes 393224 | tf_op jit(solution)/shard_map/ppermute | solution.py:564
  35.0 5.9 %collective-permute-start.8 = (f32[8,32,128]{2,1,0:T(8,128)S(1)}, f32[8,32,128]{2,1,0:T(8,128)S(1)}, u32[]{:S(2)}, u32[]{:S(2)}) collective-permute-start(f32[8,32,128]{2,1,0:T(8,128)S(1)} %collective-permute-done.7.refs_2_), channel_id=1, source_target_pairs={{0,4},{4,0},{8,12},{12,8},{24,28},{28,24},{16,20},{20,16},{1,5},{5... | collective-permute-start | bytes 393224 | tf_op jit(solution)/shard_map/ppermute | solution.py:570
  41.0 7.3 %collective-permute-start.11 = (f32[16,32,128]{2,1,0:T(8,128)S(1)}, f32[16,32,128]{2,1,0:T(8,128)S(1)}, u32[]{:S(2)}, u32[]{:S(2)}) collective-permute-start(f32[16,32,128]{2,1,0:T(8,128)S(1)} %shard_map.55), channel_id=1, source_target_pairs={{0,16},{4,20},{8,0},{12,4},{24,8},{28,12},{16,24},{20,28},{1,17},{... | collective-permute-start | bytes 786440 | tf_op jit(solution)/shard_map/ppermute | solution.py:564
  57.8 11.4 %collective-permute-start.12 = (f32[18,32,128]{2,1,0:T(8,128)S(1)}, f32[18,32,128]{2,1,0:T(8,128)S(1)}, u32[]{:S(2)}, u32[]{:S(2)}) collective-permute-start(f32[18,32,128]{2,1,0:T(8,128)S(1)} %get-tuple-element.56), channel_id=1, source_target_pairs={{0,16},{4,20},{8,0},{12,4},{24,8},{28,12},{16,24},{20,28},{1,17},{... | collective-permute-start | bytes 884744 | tf_op jit(solution)/shard_map/ppermute | solution.py:564
  60.0 6.3 %collective-permute-start.14 = (f32[9,32,128]{2,1,0:T(8,128)S(1)}, f32[9,32,128]{2,1,0:T(8,128)S(1)}, u32[]{:S(2)}, u32[]{:S(2)}) collective-permute-start(f32[9,32,128]{2,1,0:T(8,128)S(1)} %get-tuple-element.58), channel_id=1, source_target_pairs={{0,4},{4,0},{8,12},{12,8},{24,28},{28,24},{16,20},{20,16},{1,5},{5... | collective-permute-start | bytes 442376 | tf_op jit(solution)/shard_map/ppermute | solution.py:570
  61.5 7.6 %collective-permute-start.16 = (f32[9,32,128]{2,1,0:T(8,128)S(1)}, f32[9,32,128]{2,1,0:T(8,128)S(1)}, u32[]{:S(2)}, u32[]{:S(2)}) collective-permute-start(f32[9,32,128]{2,1,0:T(8,128)S(1)} %get-tuple-element.60), channel_id=1, source_target_pairs={{0,4},{4,0},{8,12},{12,8},{24,28},{28,24},{16,20},{20,16},{1,5},{5... | collective-permute-start | bytes 442376 | tf_op jit(solution)/shard_map/ppermute | solution.py:570
  66.3 7.4 %collective-permute-start.15 = (f32[9,32,128]{2,1,0:T(8,128)S(1)}, f32[9,32,128]{2,1,0:T(8,128)S(1)}, u32[]{:S(2)}, u32[]{:S(2)}) collective-permute-start(f32[9,32,128]{2,1,0:T(8,128)S(1)} %shard_map.58), channel_id=1, source_target_pairs={{0,24},{4,28},{8,16},{12,20},{24,0},{28,4},{16,8},{20,12},{1,25},{... | collective-permute-start | bytes 442376 | tf_op jit(solution)/shard_map/ppermute | solution.py:564
  69.1 7.5 %collective-permute-start.17 = (f32[9,32,128]{2,1,0:T(8,128)S(1)}, f32[9,32,128]{2,1,0:T(8,128)S(1)}, u32[]{:S(2)}, u32[]{:S(2)}) collective-permute-start(f32[9,32,128]{2,1,0:T(8,128)S(1)} %shard_map.59), channel_id=1, source_target_pairs={{0,8},{4,12},{8,24},{12,28},{24,16},{28,20},{16,0},{20,4},{1,9},{5... | collective-permute-start | bytes 442376 | tf_op jit(solution)/shard_map/ppermute | solution.py:564
  69.2 7.4 %collective-permute-start.13 = (f32[9,32,128]{2,1,0:T(8,128)S(1)}, f32[9,32,128]{2,1,0:T(8,128)S(1)}, u32[]{:S(2)}, u32[]{:S(2)}) collective-permute-start(f32[9,32,128]{2,1,0:T(8,128)S(1)} %shard_map.57), channel_id=1, source_target_pairs={{0,4},{4,0},{8,12},{12,8},{24,28},{28,24},{16,20},{20,16},{1,5},{5... | collective-permute-start | bytes 442376 | tf_op jit(solution)/shard_map/ppermute | solution.py:570
  76.7 5.9 %collective-permute-start.19 = (f32[8,32,128]{2,1,0:T(8,128)S(1)}, f32[8,32,128]{2,1,0:T(8,128)S(1)}, u32[]{:S(2)}, u32[]{:S(2)}) collective-permute-start(f32[8,32,128]{2,1,0:T(8,128)S(1)} %get-tuple-element.62.refs_0_.q0_ref), channel_id=1, source_target_pairs={{0,8},{4,12},{8,24},{12,28},{24,16},{28,20},{16,0},{20,4},{1,9},{5... | collective-permute-start | bytes 393224 | tf_op jit(solution)/shard_map/ppermute | solution.py:564
  77.3 5.9 %collective-permute-start.25 = (f32[32,128]{1,0:T(8,128)S(1)}, f32[32,128]{1,0:T(8,128)S(1)}, u32[]{:S(2)}, u32[]{:S(2)}) collective-permute-start(f32[32,128]{1,0:T(8,128)S(1)} %get-tuple-element.63.refs_0_), channel_id=1, source_target_pairs={{0,3},{1,2},{2,1},{3,0},{4,7},{5,6},{6,5},{7,4},{8,11},{9,10},{10,... | collective-permute-start | bytes 49160 | tf_op jit(solution)/shard_map/ppermute | solution.py:650
  77.3 6.8 %collective-permute-start.24 = (f32[32,128]{1,0:T(8,128)S(1)}, f32[32,128]{1,0:T(8,128)S(1)}, u32[]{:S(2)}, u32[]{:S(2)}) collective-permute-start(f32[32,128]{1,0:T(8,128)S(1)} %get-tuple-element.63.refs_0_), channel_id=1, source_target_pairs={{0,2},{1,3},{2,0},{3,1},{4,6},{5,7},{6,4},{7,5},{8,10},{9,11},{10,... | collective-permute-start | bytes 49160 | tf_op jit(solution)/shard_map/ppermute | solution.py:650
  79.2 6.6 %collective-permute-start.18 = (f32[8,32,128]{2,1,0:T(8,128)S(1)}, f32[8,32,128]{2,1,0:T(8,128)S(1)}, u32[]{:S(2)}, u32[]{:S(2)}) collective-permute-start(f32[8,32,128]{2,1,0:T(8,128)S(1)} %get-tuple-element.62.refs_0_.q0_ref), channel_id=1, source_target_pairs={{0,4},{4,0},{8,12},{12,8},{24,28},{28,24},{16,20},{20,16},{1,5},{5... | collective-permute-start | bytes 393224 | tf_op jit(solution)/shard_map/ppermute | solution.py:570
  88.5 7.2 %collective-permute-start.26 = (f32[16,32,128]{2,1,0:T(8,128)S(1)}, f32[16,32,128]{2,1,0:T(8,128)S(1)}, u32[]{:S(2)}, u32[]{:S(2)}) collective-permute-start(f32[16,32,128]{2,1,0:T(8,128)S(1)} %shard_map.62), channel_id=1, source_target_pairs={{0,16},{4,20},{8,0},{12,4},{24,8},{28,12},{16,24},{20,28},{1,17},{... | collective-permute-start | bytes 786440 | tf_op jit(solution)/shard_map/ppermute | solution.py:564
  105.8 10.2 %collective-permute-start.27 = (f32[18,32,128]{2,1,0:T(8,128)S(1)}, f32[18,32,128]{2,1,0:T(8,128)S(1)}, u32[]{:S(2)}, u32[]{:S(2)}) collective-permute-start(f32[18,32,128]{2,1,0:T(8,128)S(1)} %get-tuple-element.68), channel_id=1, source_target_pairs={{0,16},{4,20},{8,0},{12,4},{24,8},{28,12},{16,24},{20,28},{1,17},{... | collective-permute-start | bytes 884744 | tf_op jit(solution)/shard_map/ppermute | solution.py:564
  109.6 6.3 %collective-permute-start.31 = (f32[9,32,128]{2,1,0:T(8,128)S(1)}, f32[9,32,128]{2,1,0:T(8,128)S(1)}, u32[]{:S(2)}, u32[]{:S(2)}) collective-permute-start(f32[9,32,128]{2,1,0:T(8,128)S(1)} %get-tuple-element.72), channel_id=1, source_target_pairs={{0,4},{4,0},{8,12},{12,8},{24,28},{28,24},{16,20},{20,16},{1,5},{5... | collective-permute-start | bytes 442376 | tf_op jit(solution)/shard_map/ppermute | solution.py:570
  113.3 7.1 %collective-permute-start.30 = (f32[9,32,128]{2,1,0:T(8,128)S(1)}, f32[9,32,128]{2,1,0:T(8,128)S(1)}, u32[]{:S(2)}, u32[]{:S(2)}) collective-permute-start(f32[9,32,128]{2,1,0:T(8,128)S(1)} %shard_map.65), channel_id=1, source_target_pairs={{0,24},{4,28},{8,16},{12,20},{24,0},{28,4},{16,8},{20,12},{1,25},{... | collective-permute-start | bytes 442376 | tf_op jit(solution)/shard_map/ppermute | solution.py:564
  115.9 8.1 %collective-permute-start.32 = (f32[9,32,128]{2,1,0:T(8,128)S(1)}, f32[9,32,128]{2,1,0:T(8,128)S(1)}, u32[]{:S(2)}, u32[]{:S(2)}) collective-permute-start(f32[9,32,128]{2,1,0:T(8,128)S(1)} %shard_map.66), channel_id=1, source_target_pairs={{0,8},{4,12},{8,24},{12,28},{24,16},{28,20},{16,0},{20,4},{1,9},{5... | collective-permute-start | bytes 442376 | tf_op jit(solution)/shard_map/ppermute | solution.py:564
  116.0 8.0 %collective-permute-start.28 = (f32[9,32,128]{2,1,0:T(8,128)S(1)}, f32[9,32,128]{2,1,0:T(8,128)S(1)}, u32[]{:S(2)}, u32[]{:S(2)}) collective-permute-start(f32[9,32,128]{2,1,0:T(8,128)S(1)} %shard_map.64), channel_id=1, source_target_pairs={{0,4},{4,0},{8,12},{12,8},{24,28},{28,24},{16,20},{20,16},{1,5},{5... | collective-permute-start | bytes 442376 | tf_op jit(solution)/shard_map/ppermute | solution.py:570
  124.1 5.9 %collective-permute-start.34 = (f32[8,32,128]{2,1,0:T(8,128)S(1)}, f32[8,32,128]{2,1,0:T(8,128)S(1)}, u32[]{:S(2)}, u32[]{:S(2)}) collective-permute-start(f32[8,32,128]{2,1,0:T(8,128)S(1)} %get-tuple-element.74.refs_0_.p0_ref), channel_id=1, source_target_pairs={{0,8},{4,12},{8,24},{12,28},{24,16},{28,20},{16,0},{20,4},{1,9},{5... | collective-permute-start | bytes 393224 | tf_op jit(solution)/shard_map/ppermute | solution.py:564
  124.8 6.7 %collective-permute-start.40 = (f32[32,128]{1,0:T(8,128)S(1)}, f32[32,128]{1,0:T(8,128)S(1)}, u32[]{:S(2)}, u32[]{:S(2)}) collective-permute-start(f32[32,128]{1,0:T(8,128)S(1)} %get-tuple-element.75.refs_0_), channel_id=1, source_target_pairs={{0,2},{1,3},{2,0},{3,1},{4,6},{5,7},{6,4},{7,5},{8,10},{9,11},{10,... | collective-permute-start | bytes 49160 | tf_op jit(solution)/shard_map/ppermute | solution.py:650
  126.7 7.4 %collective-permute-start.33 = (f32[8,32,128]{2,1,0:T(8,128)S(1)}, f32[8,32,128]{2,1,0:T(8,128)S(1)}, u32[]{:S(2)}, u32[]{:S(2)}) collective-permute-start(f32[8,32,128]{2,1,0:T(8,128)S(1)} %get-tuple-element.74.refs_0_.p0_ref), channel_id=1, source_target_pairs={{0,4},{4,0},{8,12},{12,8},{24,28},{28,24},{16,20},{20,16},{1,5},{5... | collective-permute-start | bytes 393224 | tf_op jit(solution)/shard_map/ppermute | solution.py:570
  135.9 7.3 %collective-permute-start.38 = (f32[16,32,128]{2,1,0:T(8,128)S(1)}, f32[16,32,128]{2,1,0:T(8,128)S(1)}, u32[]{:S(2)}, u32[]{:S(2)}) collective-permute-start(f32[16,32,128]{2,1,0:T(8,128)S(1)} %shard_map.68), channel_id=1, source_target_pairs={{0,16},{4,20},{8,0},{12,4},{24,8},{28,12},{16,24},{20,28},{1,17},{... | collective-permute-start | bytes 786440 | tf_op jit(solution)/shard_map/ppermute | solution.py:564
  154.4 6.1 %collective-permute-start.47 = (f32[32,128]{1,0:T(8,128)S(1)}, f32[32,128]{1,0:T(8,128)S(1)}, u32[]{:S(2)}, u32[]{:S(2)}) collective-permute-start(f32[32,128]{1,0:T(8,128)S(1)} %shard_map.73.refs_0_), channel_id=1, source_target_pairs={{0,24},{4,28},{8,16},{12,20},{16,8},{20,12},{24,0},{28,4},{1,25},{... | collective-permute-start | bytes 49160 | tf_op jit(solution)/shard_map/ppermute | solution.py:650
  (18 other events, 99.1 us)
